TPU v7x, 128 devices: a whole 4x4x4 slice. The times are simulated.
128 devices in a mesh: dp: 16 (over y_lo, z, core), tensor: 8 (over x, y_hi).
Axes of the slice: x: 4, y: 4 (y_hi: 2, y_lo: 2; y = y_hi * 2 + y_lo), z: 4, core: 2. Of those that a mesh axis runs over, the one named last changes fastest.
Arguments:
- tokens: bfloat16 [2, 2048, 2048], P(None, 'dp'), may hold values from -6 to 6
- cotangent: bfloat16 [2, 2048, 2048], P(None, 'dp'), may hold values from -6 to 6
- pack_perm: int32 [2, 2048], replicated, may hold values from 0 to 2047, as said below
- lengths: int32 [2, 2], replicated, may hold values from 1024 to 1024, as said below
- routes: int32 [2, 2048, 8], P(None, 'dp'), may hold values from 0 to 15, all different within a row; in each aligned block of 128 rows (0 to 127, 128 to 255, ..., all dimensions but the last counted through in order) at most 80 rows name the same one
- gates: float32 [2, 2048, 8], P(None, 'dp'), may hold values from 0.06 to 0.19
- attn_gain: bfloat16 [2048], P('dp'), may hold values from 0.5 to 1.5
- w_query: bfloat16 [2048, 2048], P('dp', 'tensor'), may hold values from -0.125 to 0.125
- w_key: bfloat16 [2048, 2048], P('dp', 'tensor'), may hold values from -0.125 to 0.125
- w_value: bfloat16 [2048, 2048], P('dp', 'tensor'), may hold values from -0.125 to 0.125
- query_gain: bfloat16 [16, 128], P('tensor', 'dp'), may hold values from 0.5 to 1.5
- key_gain: bfloat16 [16, 128], P('tensor', 'dp'), may hold values from 0.5 to 1.5
- w_out: bfloat16 [2048, 2048], P('tensor', 'dp'), may hold values from -1.5 to 1.5
- moe_gain: bfloat16 [2048], P('dp'), may hold values from 0.5 to 1.5
- w_gate: bfloat16 [16, 2048, 1024], P(None, 'dp', 'tensor'), may hold values from -0.125 to 0.125
- w_up: bfloat16 [16, 2048, 1024], P(None, 'dp', 'tensor'), may hold values from -0.125 to 0.125
- w_down: bfloat16 [16, 1024, 2048], P(None, 'tensor', 'dp'), may hold values from -0.75 to 0.75
Outputs:
- output: bfloat16 [2, 2048, 2048], P(None, 'dp')
- input_grad: bfloat16 [2, 2048, 2048], P(None, 'dp')
- attn_gain_grad: float32 [2048], P('dp')
- query_grad: float32 [2048, 2048], P('dp', 'tensor')
- key_grad: float32 [2048, 2048], P('dp', 'tensor')
- value_grad: float32 [2048, 2048], P('dp', 'tensor')
- query_gain_grad: float32 [16, 128], P('tensor', 'dp')
- key_gain_grad: float32 [16, 128], P('tensor', 'dp')
- out_grad: float32 [2048, 2048], P('tensor', 'dp')
- moe_gain_grad: float32 [2048], P('dp')
- gate_grad: float32 [16, 2048, 1024], P(None, 'dp', 'tensor')
- up_grad: float32 [16, 2048, 1024], P(None, 'dp', 'tensor')
- down_grad: float32 [16, 1024, 2048], P(None, 'tensor', 'dp')
Inputs may be any that keep to these rules, and one draw needn't show every extreme that they name: `pack_perm`: each row is a permutation of the rows of its micro-batch. Every aligned block of 128 packed positions holds exactly 128 // 16 tokens from every aligned block of 128 given rows. `lengths`: each row sums to 2048. `routes`: in each aligned block of 128 rows (one index of dp in one micro-batch) an expert is named by at most 80 rows, a bound that some block reaches.
All inputs are finite; a program needn't handle non-finite values.
Results may differ from a plain program's by a relative error of at most 0.035.
Values may be sent and summed in bfloat16 or wider, within the bound.
No kernel may reach another device: no remote copies, remote signals or barrier semaphores. Data moves between devices by JAX's collectives and lax.ppermute only.
A program may use at most 256 MiB of HBM per device.

v0:
```python
import jax
import jax.numpy as jnp
from jax import lax
from jax.sharding import PartitionSpec as P

HEAD = 128


epsilon = 1e-05
rope_base = 10000.0


def rope_tables(position):
    half_dim = HEAD // 2
    frequency = rope_base ** (-(jnp.arange(half_dim, dtype=jnp.float32) * 2.0 / HEAD))
    angle = position[:, None] * frequency[None, :]
    cosine = jnp.concatenate([jnp.cos(angle), jnp.cos(angle)], axis=-1)
    sine = jnp.concatenate([jnp.sin(angle), jnp.sin(angle)], axis=-1)
    return (cosine[:, None, :], sine[:, None, :])


def rotate(values, cosine, sine):
    half_dim = values.shape[-1] // 2
    turned = jnp.concatenate([-values[..., half_dim:], values[..., :half_dim]], axis=-1)
    return values * cosine + turned * sine


def rotate_back(gradient, cosine, sine):
    half_dim = gradient.shape[-1] // 2
    scaled = gradient * sine
    turned = jnp.concatenate([scaled[..., half_dim:], -scaled[..., :half_dim]], axis=-1)
    return gradient * cosine + turned


def pack_layout(length_row, pack_total):
    seq_ends = jnp.cumsum(length_row)
    starts = seq_ends - length_row
    places = jnp.arange(pack_total, dtype=jnp.int32)
    segment = jnp.sum((places[:, None] >= seq_ends[None, :-1]).astype(jnp.int32), axis=1)
    chosen = segment[:, None] == jnp.arange(length_row.shape[0], dtype=jnp.int32)[None, :]
    start_of = jnp.sum(jnp.where(chosen, starts[None, :], 0), axis=1)
    return (segment, (places - start_of).astype(jnp.float32))


def norm_rows(values, gain):
    factor = lax.rsqrt(jnp.mean(values * values, axis=-1, keepdims=True) + epsilon)
    return (values * factor * gain, factor)


def norm_back(values, factor, gain, gradient):
    gained = gradient * gain
    inner_sum = jnp.sum(gained * values, axis=-1, keepdims=True)
    return factor * gained - values * (factor * factor * factor) * inner_sum / values.shape[-1]


def rows_inner(left_side, right_side):
    return lax.dot_general(
        left_side, right_side, (((0,), (0,)), ((), ())), preferred_element_type=jnp.float32
    )


def times_transposed(left_side, right_side):
    return lax.dot_general(
        left_side, right_side, (((1,), (1,)), ((), ())), preferred_element_type=jnp.float32
    )


def attention_scores(query_b, keys_all, visible, softmax_scale):
    scores = (
        jnp.einsum("qhd,khd->hqk", query_b, keys_all, preferred_element_type=jnp.float32)
        * softmax_scale
    )
    return jnp.where(visible[None], scores, -1e30)


def fetch_attention(shards, anchor):
    tied = lax.optimization_barrier((shards, anchor))[0]
    return (
        lax.all_gather(tied[0], "dp", axis=0, tiled=True),
        lax.all_gather(tied[1], "dp", axis=0, tiled=True),
        lax.all_gather(tied[2], "dp", axis=0, tiled=True),
        lax.all_gather(tied[3], "dp", axis=0, tiled=True),
        lax.all_gather(tied[4], "dp", axis=1, tiled=True),
        lax.all_gather(tied[5], "dp", axis=1, tiled=True),
        lax.all_gather(tied[6], "dp", axis=1, tiled=True),
    )


def fetch_experts(shards, anchor):
    tied = lax.optimization_barrier((shards, anchor))[0]
    return (
        lax.all_gather(tied[0], "dp", axis=0, tiled=True),
        lax.all_gather(tied[1], "dp", axis=1, tiled=True),
        lax.all_gather(tied[2], "dp", axis=1, tiled=True),
        lax.all_gather(tied[3], "dp", axis=2, tiled=True),
    )


def reduce_grads(grads):
    return (
        lax.psum_scatter(
            grads[0].astype(jnp.bfloat16), "dp", scatter_dimension=0, tiled=True
        ).astype(jnp.float32),
        lax.psum_scatter(
            grads[1].astype(jnp.bfloat16), "dp", scatter_dimension=0, tiled=True
        ).astype(jnp.float32),
        lax.psum_scatter(
            grads[2].astype(jnp.bfloat16), "dp", scatter_dimension=0, tiled=True
        ).astype(jnp.float32),
        lax.psum_scatter(
            grads[3].astype(jnp.bfloat16), "dp", scatter_dimension=0, tiled=True
        ).astype(jnp.float32),
        lax.psum_scatter(
            grads[4].astype(jnp.bfloat16), "dp", scatter_dimension=1, tiled=True
        ).astype(jnp.float32),
        lax.psum_scatter(
            grads[5].astype(jnp.bfloat16), "dp", scatter_dimension=1, tiled=True
        ).astype(jnp.float32),
        lax.psum_scatter(
            grads[6].astype(jnp.bfloat16), "dp", scatter_dimension=1, tiled=True
        ).astype(jnp.float32),
        lax.psum_scatter(
            grads[7].astype(jnp.bfloat16), "dp", scatter_dimension=0, tiled=True
        ).astype(jnp.float32),
        lax.psum_scatter(
            grads[8].astype(jnp.bfloat16), "dp", scatter_dimension=1, tiled=True
        ).astype(jnp.float32),
        lax.psum_scatter(
            grads[9].astype(jnp.bfloat16), "dp", scatter_dimension=1, tiled=True
        ).astype(jnp.float32),
        lax.psum_scatter(
            grads[10].astype(jnp.bfloat16), "dp", scatter_dimension=2, tiled=True
        ).astype(jnp.float32),
    )


def body(
    tokens,
    cotangent,
    pack_perm,
    lengths,
    routes,
    gates,
    attn_gain,
    w_query,
    w_key,
    w_value,
    query_gain,
    key_gain,
    w_out,
    moe_gain,
    w_gate,
    w_up,
    w_down,
):
    dp_count = lax.axis_size("dp")
    myself = lax.axis_index("dp")
    micro_count, row_count, model_width = tokens.shape
    per_pair = row_count // dp_count
    pack_total = row_count * dp_count
    top_count = routes.shape[2]
    expert_count = w_gate.shape[0]
    capacity = row_count * top_count * 5 // (4 * expert_count)
    local_width = w_query.shape[1]
    local_heads = local_width // HEAD
    softmax_scale = HEAD ** (-0.5)
    pack_blocks = pack_perm.reshape(micro_count, dp_count, row_count)
    root = pack_blocks // row_count
    arrival_order = jnp.argsort(root, axis=2, stable=True)
    grouped = arrival_order.reshape(micro_count, dp_count, dp_count, per_pair)
    from_me = lax.dynamic_index_in_dim(grouped, myself, axis=2, keepdims=False)
    given_rows = (jnp.take_along_axis(pack_blocks, from_me, axis=2) - myself * row_count).reshape(
        micro_count, row_count
    )
    own_order = lax.dynamic_index_in_dim(arrival_order, myself, axis=1, keepdims=False)
    to_slots = jnp.argsort(own_order, axis=1)
    to_given = jnp.argsort(given_rows, axis=1)
    send_tokens = jnp.take_along_axis(tokens, given_rows[:, :, None], axis=1)
    send_cotangent = jnp.take_along_axis(cotangent, given_rows[:, :, None], axis=1)
    got_tokens, got_cotangent = (
        lax.all_to_all(send_tokens, "dp", split_axis=1, concat_axis=1, tiled=True),
        lax.all_to_all(send_cotangent, "dp", split_axis=1, concat_axis=1, tiled=True),
    )
    own_tokens = jnp.take_along_axis(got_tokens, to_slots[:, :, None], axis=1)
    own_cotangent = jnp.take_along_axis(got_cotangent, to_slots[:, :, None], axis=1)
    attn_store = (attn_gain, w_query, w_key, w_value, query_gain, key_gain, w_out)
    moe_store = (moe_gain, w_gate, w_up, w_down)
    outputs = []
    input_grads = []
    grad_total = None
    for micro_index in range(micro_count):
        front_attn = fetch_attention(attn_store, own_tokens[micro_index])
        front_moe = fetch_experts(moe_store, own_tokens[micro_index])
        gain_attn, query_full, key_full, value_full, qgain_full, kgain_full, out_full = front_attn
        gain_moe, gate_full, up_full, down_full = front_moe
        segment, position = pack_layout(lengths[micro_index], pack_total)
        query_seg = lax.dynamic_slice_in_dim(segment, myself * row_count, row_count)
        own_place = lax.dynamic_slice_in_dim(position, myself * row_count, row_count)
        cosine, sine = rope_tables(own_place)
        slot_key = jnp.arange(pack_total, dtype=jnp.int32)
        slot_query = myself * row_count + jnp.arange(row_count, dtype=jnp.int32)
        visible = (query_seg[:, None] == segment[None, :]) & (
            slot_key[None, :] <= slot_query[:, None]
        )
        inputs = own_tokens[micro_index].astype(jnp.float32)
        attn_gain_f = gain_attn.astype(jnp.float32)
        normed, attn_factor = norm_rows(inputs, attn_gain_f)
        normed_b = normed.astype(jnp.bfloat16)
        query_pre = jnp.dot(normed_b, query_full, preferred_element_type=jnp.float32)
        key_pre = jnp.dot(normed_b, key_full, preferred_element_type=jnp.float32)
        value_b = (
            jnp.dot(normed_b, value_full, preferred_element_type=jnp.float32)
            .astype(jnp.bfloat16)
            .reshape(row_count, local_heads, HEAD)
        )
        query_sq, key_sq = lax.psum(
            (jnp.sum(query_pre * query_pre, axis=1), jnp.sum(key_pre * key_pre, axis=1)), "tensor"
        )
        query_factor = lax.rsqrt(query_sq / model_width + epsilon)[:, None]
        key_factor = lax.rsqrt(key_sq / model_width + epsilon)[:, None]
        query_scale = qgain_full.reshape(local_width).astype(jnp.float32)
        key_scale = kgain_full.reshape(local_width).astype(jnp.float32)
        query_b = rotate(
            (query_pre * query_factor * query_scale).reshape(row_count, local_heads, HEAD),
            cosine,
            sine,
        ).astype(jnp.bfloat16)
        key_b = rotate(
            (key_pre * key_factor * key_scale).reshape(row_count, local_heads, HEAD), cosine, sine
        ).astype(jnp.bfloat16)
        keys_all, values_all = (
            lax.all_gather(key_b, "dp", axis=0, tiled=True),
            lax.all_gather(value_b, "dp", axis=0, tiled=True),
        )
        scores = attention_scores(query_b, keys_all, visible, softmax_scale)
        peak = jnp.max(scores, axis=-1, keepdims=True)
        log_total = peak + jnp.log(jnp.sum(jnp.exp(scores - peak), axis=-1, keepdims=True))
        probs_b = jnp.exp(scores - log_total).astype(jnp.bfloat16)
        mixed = jnp.einsum("hqk,khd->qhd", probs_b, values_all, preferred_element_type=jnp.float32)
        mixed_b = mixed.astype(jnp.bfloat16).reshape(row_count, local_width)
        attn_out = lax.psum(
            jnp.dot(mixed_b, out_full, preferred_element_type=jnp.float32), "tensor"
        )
        hidden_one = inputs + attn_out
        moe_gain_f = gain_moe.astype(jnp.float32)
        moe_normed, moe_factor = norm_rows(hidden_one, moe_gain_f)
        moe_in = moe_normed.astype(jnp.bfloat16)
        flat_routes = routes[micro_index].reshape(-1)
        hot_table = (
            flat_routes[:, None] == jnp.arange(expert_count, dtype=jnp.int32)[None, :]
        ).astype(jnp.int32)
        slot_rank = jnp.sum((jnp.cumsum(hot_table, axis=0) - hot_table) * hot_table, axis=1)
        target = flat_routes * capacity + slot_rank
        route_owner = jnp.arange(row_count * top_count, dtype=jnp.int32) // top_count
        owner_row = (
            jnp.full((expert_count * capacity,), row_count, jnp.int32).at[target].set(route_owner)
        )
        slot_gate = (
            jnp.zeros((expert_count * capacity,), jnp.float32)
            .at[target]
            .set(gates[micro_index].reshape(-1))
        )
        padded_in = jnp.concatenate([moe_in, jnp.zeros((1, model_width), jnp.bfloat16)], axis=0)
        expert_in = padded_in[owner_row].reshape(expert_count, capacity, model_width)
        gate_h = jnp.einsum(
            "ecd,edf->ecf", expert_in, gate_full, preferred_element_type=jnp.float32
        )
        up_h = jnp.einsum("ecd,edf->ecf", expert_in, up_full, preferred_element_type=jnp.float32)
        sigmoid_gate = jax.nn.sigmoid(gate_h)
        active = gate_h * sigmoid_gate
        hidden_b = (active * up_h).astype(jnp.bfloat16)
        expert_out = (
            jnp.einsum(
                "ecf,efd->ecd", hidden_b, down_full, preferred_element_type=jnp.float32
            ).reshape(expert_count * capacity, model_width)
            * slot_gate[:, None]
        )
        moe_part = jnp.sum(expert_out[target].reshape(row_count, top_count, model_width), axis=1)
        moe_out = lax.psum(moe_part.astype(jnp.bfloat16), "tensor").astype(jnp.float32)
        outputs.append((hidden_one + moe_out).astype(jnp.bfloat16))
        back_attn = fetch_attention(attn_store, moe_out)
        back_moe = fetch_experts(moe_store, moe_out)
        gain_attn, query_full, key_full, value_full, qgain_full, kgain_full, out_full = back_attn
        gain_moe, gate_full, up_full, down_full = back_moe
        upstream = own_cotangent[micro_index].astype(jnp.float32)
        padded_up = jnp.concatenate([upstream, jnp.zeros((1, model_width), jnp.float32)], axis=0)
        delta_out = (
            (padded_up[owner_row] * slot_gate[:, None])
            .astype(jnp.bfloat16)
            .reshape(expert_count, capacity, model_width)
        )
        grad_down = jnp.einsum(
            "ecf,ecd->efd", hidden_b, delta_out, preferred_element_type=jnp.float32
        )
        delta_hidden = jnp.einsum(
            "ecd,efd->ecf", delta_out, down_full, preferred_element_type=jnp.float32
        )
        delta_gate = (
            delta_hidden * up_h * sigmoid_gate * (1.0 + gate_h * (1.0 - sigmoid_gate))
        ).astype(jnp.bfloat16)
        delta_up = (delta_hidden * active).astype(jnp.bfloat16)
        grad_gate = jnp.einsum(
            "ecd,ecf->edf", expert_in, delta_gate, preferred_element_type=jnp.float32
        )
        grad_up = jnp.einsum(
            "ecd,ecf->edf", expert_in, delta_up, preferred_element_type=jnp.float32
        )
        delta_in = jnp.einsum(
            "ecf,edf->ecd", delta_gate, gate_full, preferred_element_type=jnp.float32
        )
        delta_in = (
            delta_in
            + jnp.einsum("ecf,edf->ecd", delta_up, up_full, preferred_element_type=jnp.float32)
        ).reshape(expert_count * capacity, model_width)
        moe_grad_part = jnp.sum(delta_in[target].reshape(row_count, top_count, model_width), axis=1)
        moe_grad = lax.psum(moe_grad_part.astype(jnp.bfloat16), "tensor").astype(jnp.float32)
        grad_moe_gain = jnp.sum(moe_grad * hidden_one * moe_factor, axis=0)
        delta_one = upstream + norm_back(hidden_one, moe_factor, moe_gain_f, moe_grad)
        delta_attn = delta_one.astype(jnp.bfloat16)
        grad_out = rows_inner(mixed_b, delta_attn)
        delta_mixed = (
            times_transposed(delta_attn, out_full)
            .astype(jnp.bfloat16)
            .reshape(row_count, local_heads, HEAD)
        )
        again_scores = attention_scores(query_b, keys_all, visible, softmax_scale)
        probs = jnp.exp(again_scores - log_total)
        probs_low = probs.astype(jnp.bfloat16)
        delta_probs = jnp.einsum(
            "qhd,khd->hqk", delta_mixed, values_all, preferred_element_type=jnp.float32
        )
        delta_scores = (
            probs * (delta_probs - jnp.sum(probs * delta_probs, axis=-1, keepdims=True))
        ).astype(jnp.bfloat16)
        delta_query = (
            jnp.einsum("hqk,khd->qhd", delta_scores, keys_all, preferred_element_type=jnp.float32)
            * softmax_scale
        )
        key_term = (
            jnp.einsum("hqk,qhd->khd", delta_scores, query_b, preferred_element_type=jnp.float32)
            * softmax_scale
        )
        value_term = jnp.einsum(
            "hqk,qhd->khd", probs_low, delta_mixed, preferred_element_type=jnp.float32
        )
        delta_key, delta_value = (
            lax.psum_scatter(
                key_term.astype(jnp.bfloat16), "dp", scatter_dimension=0, tiled=True
            ).astype(jnp.float32),
            lax.psum_scatter(
                value_term.astype(jnp.bfloat16), "dp", scatter_dimension=0, tiled=True
            ).astype(jnp.float32),
        )
        delta_qnorm = rotate_back(delta_query, cosine, sine).reshape(row_count, local_width)
        delta_knorm = rotate_back(delta_key, cosine, sine).reshape(row_count, local_width)
        grad_qgain = jnp.sum(delta_qnorm * query_pre * query_factor, axis=0).reshape(
            local_heads, HEAD
        )
        grad_kgain = jnp.sum(delta_knorm * key_pre * key_factor, axis=0).reshape(local_heads, HEAD)
        weighted_query = delta_qnorm * query_scale
        weighted_key = delta_knorm * key_scale
        inner_query, inner_key = lax.psum(
            (jnp.sum(weighted_query * query_pre, axis=1), jnp.sum(weighted_key * key_pre, axis=1)),
            "tensor",
        )
        delta_qpre = (
            query_factor * weighted_query
            - query_pre
            * (query_factor * query_factor * query_factor)
            * inner_query[:, None]
            / model_width
        ).astype(jnp.bfloat16)
        delta_kpre = (
            key_factor * weighted_key
            - key_pre * (key_factor * key_factor * key_factor) * inner_key[:, None] / model_width
        ).astype(jnp.bfloat16)
        delta_vlow = delta_value.reshape(row_count, local_width).astype(jnp.bfloat16)
        grad_query = rows_inner(normed_b, delta_qpre)
        grad_key = rows_inner(normed_b, delta_kpre)
        grad_value = rows_inner(normed_b, delta_vlow)
        attn_grad_part = (
            times_transposed(delta_qpre, query_full)
            + times_transposed(delta_kpre, key_full)
            + times_transposed(delta_vlow, value_full)
        )
        attn_grad = lax.psum(attn_grad_part.astype(jnp.bfloat16), "tensor").astype(jnp.float32)
        grad_attn_gain = jnp.sum(attn_grad * inputs * attn_factor, axis=0)
        input_grads.append(
            (delta_one + norm_back(inputs, attn_factor, attn_gain_f, attn_grad)).astype(
                jnp.bfloat16
            )
        )
        grads = (
            grad_attn_gain,
            grad_query,
            grad_key,
            grad_value,
            grad_qgain,
            grad_kgain,
            grad_out,
            grad_moe_gain,
            grad_gate,
            grad_up,
            grad_down,
        )
        grad_total = grads if grad_total is None else jax.tree.map(jnp.add, grad_total, grads)
    grad_total = reduce_grads(grad_total)
    out_back = jnp.take_along_axis(jnp.stack(outputs), own_order[:, :, None], axis=1)
    grad_back = jnp.take_along_axis(jnp.stack(input_grads), own_order[:, :, None], axis=1)
    out_home, grad_home = (
        lax.all_to_all(out_back, "dp", split_axis=1, concat_axis=1, tiled=True),
        lax.all_to_all(grad_back, "dp", split_axis=1, concat_axis=1, tiled=True),
    )
    output = jnp.take_along_axis(out_home, to_given[:, :, None], axis=1)
    input_grad = jnp.take_along_axis(grad_home, to_given[:, :, None], axis=1)
    return (output, input_grad) + tuple(grad_total)


def solution(mesh):
    placed = (
        P(None, "dp", None),
        P(None, "dp", None),
        P(),
        P(),
        P(None, "dp", None),
        P(None, "dp", None),
        P("dp"),
        P("dp", "tensor"),
        P("dp", "tensor"),
        P("dp", "tensor"),
        P("tensor", "dp"),
        P("tensor", "dp"),
        P("tensor", "dp"),
        P("dp"),
        P(None, "dp", "tensor"),
        P(None, "dp", "tensor"),
        P(None, "tensor", "dp"),
    )
    return jax.shard_map(
        body,
        mesh=mesh,
        in_specs=placed,
        out_specs=(
            P(None, "dp", None),
            P(None, "dp", None),
            P("dp"),
            P("dp", "tensor"),
            P("dp", "tensor"),
            P("dp", "tensor"),
            P("tensor", "dp"),
            P("tensor", "dp"),
            P("tensor", "dp"),
            P("dp"),
            P(None, "dp", "tensor"),
            P(None, "dp", "tensor"),
            P(None, "tensor", "dp"),
        ),
        check_vma=False,
    )
```

profile of v0, /device:TPU:0, one launch (start us, length us, event | category | flops | bytes accessed | tf_op | source)
XLA Modules:
  0.0 3047.3 jit_solution(5445544129113201964)
XLA Ops:
  36.9 22.8 all_to_all.20
  90.4 17.0 all-gather.4
  107.4 16.7 all-gather.6
  124.4 17.0 all-gather.5
  153.9 23.9 all-reduce.11
  196.1 25.1 all-gather.67.cloned.1.call-done
  223.3 34.3 %all-gather.61.cloned.1.call-done = bf16[2048,2,128]{0,2,1:T(8,128)(2,1)} async-done(((bf16[128,2,128]{0,2,1:T(8,128)(2,1)}), bf16[2048,2,128]{0,2,1:T(8,128)(2,1)}) %all-gather.61.cloned.1.call-update) | async-done | bytes 1048592 | tf_op jit(solution)/shard_map/all_gather | solution.py:233
  259.4 34.1 %all-gather.69.cloned.1.call-done = bf16[256,2048]{1,0:T(8,128)(2,1)} async-done(((bf16[256,128]{1,0:T(8,128)(2,1)}), bf16[256,2048]{1,0:T(8,128)(2,1)}) %all-gather.69.cloned.1.call-update) | async-done | bytes 1048592 | tf_op jit(solution)/shard_map/all_gather | solution.py:85
  313.6 18.0 all-gather.7
  331.6 53.8 %all-reduce.26.cloned.1.call-done = f32[128,2048]{1,0:T(8,128)} async-done(((f32[128,2048]{1,0:T(8,128)}), f32[128,2048]{1,0:T(8,128)}) %all-reduce.26.cloned.1.call-update) | async-done | bytes 1048592 | tf_op jit(solution)/shard_map/psum | solution.py:241
  394.2 42.9 %all-gather.71.cloned.1.call-done = bf16[16,2048,128]{2,1,0:T(8,128)(2,1)} async-done(((bf16[16,128,128]{2,1,0:T(8,128)(2,1)}), bf16[16,2048,128]{2,1,0:T(8,128)(2,1)}) %all-gather.71.cloned.1.call-update) | async-done | bytes 8388624 | tf_op jit(solution)/shard_map/all_gather | solution.py:93
  443.7 48.3 %all-gather.73.cloned.1.call-done = bf16[16,2048,128]{2,1,0:T(8,128)(2,1)} async-done(((bf16[16,128,128]{2,1,0:T(8,128)(2,1)}), bf16[16,2048,128]{2,1,0:T(8,128)(2,1)}) %all-gather.73.cloned.1.call-update) | async-done | bytes 8388624 | tf_op jit(solution)/shard_map/all_gather | solution.py:94
  498.7 56.7 %all-gather.75.cloned.1.call-done = bf16[16,128,2048]{2,1,0:T(8,128)(2,1)} async-done(((bf16[16,128,128]{2,1,0:T(8,128)(2,1)}), bf16[16,128,2048]{2,1,0:T(8,128)(2,1)}) %all-gather.75.cloned.1.call-update) | async-done | bytes 8388624 | tf_op jit(solution)/shard_map/all_gather | solution.py:95
  565.0 13.0 gather_fusion.3
  584.3 85.0 %all-reduce.28.cloned.1.call-done = bf16[128,2048]{1,0:T(8,128)(2,1)} async-done(((bf16[128,2048]{1,0:T(8,128)(2,1)}), bf16[128,2048]{1,0:T(8,128)(2,1)}) %all-reduce.28.cloned.1.call-update) | async-done | bytes 524304 | tf_op jit(solution)/shard_map/psum | solution.py:279
  679.4 50.0 %all-gather.91.cloned.1.call-done = bf16[16,128,2048]{2,1,0:T(8,128)(2,1)} async-done(((bf16[16,128,128]{2,1,0:T(8,128)(2,1)}), bf16[16,128,2048]{2,1,0:T(8,128)(2,1)}) %all-gather.91.cloned.1.call-update) | async-done | bytes 8388624 | tf_op jit(solution)/shard_map/all_gather | solution.py:95
  739.0 43.7 %all-gather.93.cloned.1.call-done = bf16[16,2048,128]{2,1,0:T(8,128)(2,1)} async-done(((bf16[16,128,128]{2,1,0:T(8,128)(2,1)}), bf16[16,2048,128]{2,1,0:T(8,128)(2,1)}) %all-gather.93.cloned.1.call-update) | async-done | bytes 8388624 | tf_op jit(solution)/shard_map/all_gather | solution.py:93
  793.0 44.3 %all-gather.95.cloned.1.call-done = bf16[16,2048,128]{2,1,0:T(8,128)(2,1)} async-done(((bf16[16,128,128]{2,1,0:T(8,128)(2,1)}), bf16[16,2048,128]{2,1,0:T(8,128)(2,1)}) %all-gather.95.cloned.1.call-update) | async-done | bytes 8388624 | tf_op jit(solution)/shard_map/all_gather | solution.py:94
  837.4 13.5 convolution_add_fusion
  871.0 85.8 %all-reduce.34.cloned.1.call-done = bf16[128,2048]{1,0:T(8,128)(2,1)} async-done(((bf16[128,2048]{1,0:T(8,128)(2,1)}), bf16[128,2048]{1,0:T(8,128)(2,1)}) %all-reduce.34.cloned.1.call-update) | async-done | bytes 524304 | tf_op jit(solution)/shard_map/psum | solution.py:316
  961.7 28.6 all-gather.97.cloned.1.call-done
  1010.9 48.2 %reduce-scatter.24.cloned.1.call-done = bf16[128,2,128]{2,0,1:T(8,128)(2,1)} async-done(((bf16[2048,2,128]{2,0,1:T(8,128)(2,1)}), bf16[128,2,128]{2,0,1:T(8,128)(2,1)}) %reduce-scatter.24.cloned.1.call-update) | async-done | bytes 65552 | tf_op jit(solution)/shard_map/reduce_scatter | solution.py:347
  1061.8 23.9 all-reduce.10
  1093.6 32.6 %all-gather.101.cloned.1.call-done = bf16[2048,256]{1,0:T(8,128)(2,1)} async-done(((bf16[128,256]{1,0:T(8,128)(2,1)}), bf16[2048,256]{1,0:T(8,128)(2,1)}) %all-gather.101.cloned.1.call-update) | async-done | bytes 1048592 | tf_op jit(solution)/shard_map/all_gather | solution.py:81
  1127.9 32.5 %all-gather.103.cloned.1.call-done = bf16[2048,256]{1,0:T(8,128)(2,1)} async-done(((bf16[128,256]{1,0:T(8,128)(2,1)}), bf16[2048,256]{1,0:T(8,128)(2,1)}) %all-gather.103.cloned.1.call-update) | async-done | bytes 1048592 | tf_op jit(solution)/shard_map/all_gather | solution.py:82
  1160.4 64.1 %reduce-scatter.38.cloned.1.call-done = bf16[128,256]{1,0:T(8,128)(2,1)} async-done(((bf16[2048,256]{1,0:T(8,128)(2,1)}), bf16[128,256]{1,0:T(8,128)(2,1)}) %reduce-scatter.38.cloned.1.call-update) | async-done | bytes 65552 | tf_op jit(solution)/shard_map/convert_element_type | solution.py:377
  1231.7 16.2 all-gather
  1247.9 17.8 all-gather.2
  1265.9 16.3 all-gather.1
  1282.5 28.7 all-reduce.36.cloned.1.call-done
  1313.8 29.6 all-gather.47.cloned.1.call-done
  1345.0 32.4 %all-gather.45.cloned.1.call-done = bf16[2048,256]{1,0:T(8,128)(2,1)} async-done(((bf16[128,256]{1,0:T(8,128)(2,1)}), bf16[2048,256]{1,0:T(8,128)(2,1)}) %all-gather.45.cloned.1.call-update) | async-done | bytes 1048592 | tf_op jit(solution)/shard_map/all_gather | solution.py:80
  1379.2 23.9 all-reduce.9
  1414.6 31.8 %all-gather.49.cloned.1.call-done = bf16[2048,2,128]{2,0,1:T(8,128)(2,1)} async-done(((bf16[128,2,128]{2,0,1:T(8,128)(2,1)}), bf16[2048,2,128]{2,0,1:T(8,128)(2,1)}) %all-gather.49.cloned.1.call-update) | async-done | bytes 1048592 | tf_op jit(solution)/shard_map/all_gather | solution.py:232
  1448.5 34.2 %all-gather.43.cloned.1.call-done = bf16[2048,2,128]{0,2,1:T(8,128)(2,1)} async-done(((bf16[128,2,128]{0,2,1:T(8,128)(2,1)}), bf16[2048,2,128]{0,2,1:T(8,128)(2,1)}) %all-gather.43.cloned.1.call-update) | async-done | bytes 1048592 | tf_op jit(solution)/shard_map/all_gather | solution.py:233
  1484.4 33.9 %all-gather.51.cloned.1.call-done = bf16[256,2048]{1,0:T(8,128)(2,1)} async-done(((bf16[256,128]{1,0:T(8,128)(2,1)}), bf16[256,2048]{1,0:T(8,128)(2,1)}) %all-gather.51.cloned.1.call-update) | async-done | bytes 1048592 | tf_op jit(solution)/shard_map/all_gather | solution.py:85
  1537.9 17.9 all-gather.3
  1555.8 54.2 %all-reduce.22.cloned.1.call-done = f32[128,2048]{1,0:T(8,128)} async-done(((f32[128,2048]{1,0:T(8,128)}), f32[128,2048]{1,0:T(8,128)}) %all-reduce.22.cloned.1.call-update) | async-done | bytes 1048592 | tf_op jit(solution)/shard_map/psum | solution.py:241
  1618.9 42.9 %all-gather.53.cloned.1.call-done = bf16[16,2048,128]{2,1,0:T(8,128)(2,1)} async-done(((bf16[16,128,128]{2,1,0:T(8,128)(2,1)}), bf16[16,2048,128]{2,1,0:T(8,128)(2,1)}) %all-gather.53.cloned.1.call-update) | async-done | bytes 8388624 | tf_op jit(solution)/shard_map/all_gather | solution.py:93
  1668.5 48.1 %all-gather.55.cloned.1.call-done = bf16[16,2048,128]{2,1,0:T(8,128)(2,1)} async-done(((bf16[16,128,128]{2,1,0:T(8,128)(2,1)}), bf16[16,2048,128]{2,1,0:T(8,128)(2,1)}) %all-gather.55.cloned.1.call-update) | async-done | bytes 8388624 | tf_op jit(solution)/shard_map/all_gather | solution.py:94
  1724.0 55.9 %all-gather.57.cloned.1.call-done = bf16[16,128,2048]{2,1,0:T(8,128)(2,1)} async-done(((bf16[16,128,128]{2,1,0:T(8,128)(2,1)}), bf16[16,128,2048]{2,1,0:T(8,128)(2,1)}) %all-gather.57.cloned.1.call-update) | async-done | bytes 8388624 | tf_op jit(solution)/shard_map/all_gather | solution.py:95
  1789.6 13.0 gather_fusion.1
  1808.9 85.0 %all-reduce.24.cloned.1.call-done = bf16[128,2048]{1,0:T(8,128)(2,1)} async-done(((bf16[128,2048]{1,0:T(8,128)(2,1)}), bf16[128,2048]{1,0:T(8,128)(2,1)}) %all-reduce.24.cloned.1.call-update) | async-done | bytes 524304 | tf_op jit(solution)/shard_map/psum | solution.py:279
  1902.8 51.4 %all-gather.77.cloned.1.call-done = bf16[16,128,2048]{2,1,0:T(8,128)(2,1)} async-done(((bf16[16,128,128]{2,1,0:T(8,128)(2,1)}), bf16[16,128,2048]{2,1,0:T(8,128)(2,1)}) %all-gather.77.cloned.1.call-update) | async-done | bytes 8388624 | tf_op jit(solution)/shard_map/all_gather | solution.py:95
  1963.7 43.8 %all-gather.79.cloned.1.call-done = bf16[16,2048,128]{2,1,0:T(8,128)(2,1)} async-done(((bf16[16,128,128]{2,1,0:T(8,128)(2,1)}), bf16[16,2048,128]{2,1,0:T(8,128)(2,1)}) %all-gather.79.cloned.1.call-update) | async-done | bytes 8388624 | tf_op jit(solution)/shard_map/all_gather | solution.py:93
  2017.8 44.7 %all-gather.81.cloned.1.call-done = bf16[16,2048,128]{2,1,0:T(8,128)(2,1)} async-done(((bf16[16,128,128]{2,1,0:T(8,128)(2,1)}), bf16[16,2048,128]{2,1,0:T(8,128)(2,1)}) %all-gather.81.cloned.1.call-update) | async-done | bytes 8388624 | tf_op jit(solution)/shard_map/all_gather | solution.py:94
  2062.4 13.3 convolution_add_fusion.1
  2095.8 85.8 %all-reduce.30.cloned.1.call-done = bf16[128,2048]{1,0:T(8,128)(2,1)} async-done(((bf16[128,2048]{1,0:T(8,128)(2,1)}), bf16[128,2048]{1,0:T(8,128)(2,1)}) %all-reduce.30.cloned.1.call-update) | async-done | bytes 524304 | tf_op jit(solution)/shard_map/psum | solution.py:316
  2186.5 28.7 all-gather.83.cloned.1.call-done
  2237.9 47.2 %reduce-scatter.22.cloned.1.call-done = bf16[128,2,128]{2,0,1:T(8,128)(2,1)} async-done(((bf16[2048,2,128]{2,0,1:T(8,128)(2,1)}), bf16[128,2,128]{2,0,1:T(8,128)(2,1)}) %reduce-scatter.22.cloned.1.call-update) | async-done | bytes 65552 | tf_op jit(solution)/shard_map/reduce_scatter | solution.py:347
  2287.7 23.8 all-reduce.8
  2319.8 32.5 %all-gather.87.cloned.1.call-done = bf16[2048,256]{1,0:T(8,128)(2,1)} async-done(((bf16[128,256]{1,0:T(8,128)(2,1)}), bf16[2048,256]{1,0:T(8,128)(2,1)}) %all-gather.87.cloned.1.call-update) | async-done | bytes 1048592 | tf_op jit(solution)/shard_map/all_gather | solution.py:81
  2354.0 32.6 %all-gather.89.cloned.1.call-done = bf16[2048,256]{1,0:T(8,128)(2,1)} async-done(((bf16[128,256]{1,0:T(8,128)(2,1)}), bf16[2048,256]{1,0:T(8,128)(2,1)}) %all-gather.89.cloned.1.call-update) | async-done | bytes 1048592 | tf_op jit(solution)/shard_map/all_gather | solution.py:82
  2386.7 64.0 %reduce-scatter.36.cloned.1.call-done = bf16[128,256]{1,0:T(8,128)(2,1)} async-done(((bf16[2048,256]{1,0:T(8,128)(2,1)}), bf16[128,256]{1,0:T(8,128)(2,1)}) %reduce-scatter.36.cloned.1.call-update) | async-done | bytes 65552 | tf_op jit(solution)/shard_map/convert_element_type | solution.py:377
  2468.0 14.5 add_convert_fusion
  2592.8 16.8 all-to-all-done.3
  2614.0 21.3 reduce-scatter.42.cloned.1.call-done
  2638.0 61.3 %reduce-scatter.40.cloned.1.call-done = bf16[128,256]{1,0:T(8,128)(2,1)} async-done(((bf16[2048,256]{1,0:T(8,128)(2,1)}), bf16[128,256]{1,0:T(8,128)(2,1)}) %reduce-scatter.40.cloned.1.call-update) | async-done | bytes 65552
  2701.0 28.4 all-reduce.12
  2746.3 15.7 reduce-scatter.26.cloned.1.call-done
  2763.5 60.7 %reduce-scatter.28.cloned.1.call-done = bf16[128,256]{1,0:T(8,128)(2,1)} async-done(((bf16[2048,256]{1,0:T(8,128)(2,1)}), bf16[128,256]{1,0:T(8,128)(2,1)}) %reduce-scatter.28.cloned.1.call-update) | async-done | bytes 65552 | tf_op jit(solution)/shard_map/reduce_scatter | solution.py:107
  2825.7 61.0 %reduce-scatter.30.cloned.1.call-done = bf16[128,256]{1,0:T(8,128)(2,1)} async-done(((bf16[2048,256]{1,0:T(8,128)(2,1)}), bf16[128,256]{1,0:T(8,128)(2,1)}) %reduce-scatter.30.cloned.1.call-update) | async-done | bytes 65552 | tf_op jit(solution)/shard_map/reduce_scatter | solution.py:110
  2888.1 74.1 %reduce-scatter.32.cloned.1.call-done = bf16[16,128,128]{2,1,0:T(8,128)(2,1)} async-done(((bf16[16,2048,128]{2,1,0:T(8,128)(2,1)}), bf16[16,128,128]{2,1,0:T(8,128)(2,1)}) %reduce-scatter.32.cloned.1.call-update) | async-done | bytes 524304 | tf_op jit(solution)/shard_map/reduce_scatter | solution.py:125
  2964.4 73.5 %reduce-scatter.34.cloned.1.call-done = bf16[16,128,128]{2,1,0:T(8,128)(2,1)} async-done(((bf16[16,2048,128]{2,1,0:T(8,128)(2,1)}), bf16[16,128,128]{2,1,0:T(8,128)(2,1)}) %reduce-scatter.34.cloned.1.call-update) | async-done | bytes 524304 | tf_op jit(solution)/shard_map/reduce_scatter | solution.py:128
  (624 shorter events, 576.1 us)
Async XLA Ops:
  59.7 20.2 all-to-all-start
  65.2 76.4 %all-gather.63.cloned.1.call-start = ((), (), s32[]{:S(2)}) async-start(), calls=%async_computation.28 | async-start | bytes 1114112 | tf_op jit(solution)/shard_map/all_gather | solution.py:80
  85.8 299.6 %copy-start.7 = (bf16[2,128,2048]{2,1,0:T(8,128)(2,1)}, bf16[2,128,2048]{2,1,0:T(8,128)(2,1)S(1)}, u32[]{:S(2)}) copy-start(bf16[2,128,2048]{2,1,0:T(8,128)(2,1)S(1)} %get-tuple-element.212) | copy-start | bytes 3145732
  85.8 66.4 %all-gather.65.cloned.1.call-start = ((), (), s32[]{:S(2)}) async-start(), calls=%async_computation.29 | async-start | bytes 1114112 | tf_op jit(solution)/shard_map/all_gather | solution.py:81
  86.4 104.4 %all-gather.59.cloned.1.call-start = ((), (), s32[]{:S(2)}) async-start(), calls=%async_computation.26 | async-start | bytes 1114112 | tf_op jit(solution)/shard_map/all_gather | solution.py:82
  89.8 131.4 %all-gather.67.cloned.1.call-start = ((), (), s32[]{:S(2)}) async-start(), calls=%async_computation.30 | async-start | bytes 1114112 | tf_op jit(solution)/shard_map/all_gather | solution.py:232
  179.6 78.0 %all-gather.61.cloned.1.call-start = ((), (), s32[]{:S(2)}) async-start(), calls=%async_computation.27 | async-start | bytes 1114112 | tf_op jit(solution)/shard_map/all_gather | solution.py:233
  193.2 100.3 %all-gather.69.cloned.1.call-start = ((), (), s32[]{:S(2)}) async-start(), calls=%async_computation.31 | async-start | bytes 1114112 | tf_op jit(solution)/shard_map/all_gather | solution.py:85
  193.9 191.5 %all-reduce.26.cloned.1.call-start = ((), (), s32[]{:S(2)}) async-start(), calls=%async_computation.32 | async-start | bytes 2097152 | tf_op jit(solution)/shard_map/psum | solution.py:241
  296.0 141.1 %all-gather.71.cloned.1.call-start = ((), (), s32[]{:S(2)}) async-start(), calls=%async_computation.33 | async-start | bytes 8912896 | tf_op jit(solution)/shard_map/all_gather | solution.py:93
  296.6 195.4 %all-gather.73.cloned.1.call-start = ((), (), s32[]{:S(2)}) async-start(), calls=%async_computation.34 | async-start | bytes 8912896 | tf_op jit(solution)/shard_map/all_gather | solution.py:94
  297.4 258.1 %all-gather.75.cloned.1.call-start = ((), (), s32[]{:S(2)}) async-start(), calls=%async_computation.35 | async-start | bytes 8912896 | tf_op jit(solution)/shard_map/all_gather | solution.py:95
  297.9 371.4 %all-reduce.28.cloned.1.call-start = ((), (), s32[]{:S(2)}) async-start(), calls=%async_computation.36 | async-start | bytes 1048576 | tf_op jit(solution)/shard_map/psum | solution.py:279
  584.2 145.2 %all-gather.91.cloned.1.call-start = ((), (), s32[]{:S(2)}) async-start(), calls=%async_computation.47 | async-start | bytes 8912896 | tf_op jit(solution)/shard_map/all_gather | solution.py:95
  669.4 113.3 %all-gather.93.cloned.1.call-start = ((), (), s32[]{:S(2)}) async-start(), calls=%async_computation.48 | async-start | bytes 8912896 | tf_op jit(solution)/shard_map/all_gather | solution.py:93
  669.9 167.4 %all-gather.95.cloned.1.call-start = ((), (), s32[]{:S(2)}) async-start(), calls=%async_computation.49 | async-start | bytes 8912896 | tf_op jit(solution)/shard_map/all_gather | solution.py:94
  670.5 286.2 %all-reduce.34.cloned.1.call-start = ((), (), s32[]{:S(2)}) async-start(), calls=%async_computation.50 | async-start | bytes 1048576 | tf_op jit(solution)/shard_map/psum | solution.py:316
  870.2 120.1 %all-gather.97.cloned.1.call-start = ((), (), s32[]{:S(2)}) async-start(), calls=%async_computation.51 | async-start | bytes 1114112 | tf_op jit(solution)/shard_map/all_gather | solution.py:85
  870.8 188.4 %reduce-scatter.24.cloned.1.call-start = ((), (), s32[]{:S(2)}) async-start(), calls=%async_computation.53 | async-start | bytes 1114112 | tf_op jit(solution)/shard_map/reduce_scatter | solution.py:347
  997.4 94.5 %all-gather.99.cloned.1.call-start = ((), (), s32[]{:S(2)}) async-start(), calls=%async_computation.52 | async-start | bytes 1114112 | tf_op jit(solution)/shard_map/all_gather | solution.py:80
  998.0 128.2 %all-gather.101.cloned.1.call-start = ((), (), s32[]{:S(2)}) async-start(), calls=%async_computation.54 | async-start | bytes 1114112 | tf_op jit(solution)/shard_map/all_gather | solution.py:81
  998.7 161.7 %all-gather.103.cloned.1.call-start = ((), (), s32[]{:S(2)}) async-start(), calls=%async_computation.55 | async-start | bytes 1114112 | tf_op jit(solution)/shard_map/all_gather | solution.py:82
  999.5 225.0 %reduce-scatter.38.cloned.1.call-start = ((), (), s32[]{:S(2)}) async-start(), calls=%async_computation.63 | async-start | bytes 1114112 | tf_op jit(solution)/shard_map/convert_element_type | solution.py:377
  1006.4 304.9 %copy-start.8 = (bf16[2,128,2048]{2,1,0:T(8,128)(2,1)S(1)}, bf16[2,128,2048]{2,1,0:T(8,128)(2,1)}, u32[]{:S(2)}) copy-start(bf16[2,128,2048]{2,1,0:T(8,128)(2,1)} %copy-done.7) | copy-start | bytes 3145732
  1006.4 304.9 %copy-start.61 = (f32[16,1,128]{2,1,0:T(1,128)S(1)}, f32[16,1,128]{2,1,0:T(1,128)}, u32[]{:S(2)}) copy-start(f32[16,1,128]{2,1,0:T(1,128)} %copy-done.60) | copy-start | bytes 24580
  1006.4 304.8 %all-reduce.36.cloned.1.call-start = ((), (), s32[]{:S(2)}) async-start(), calls=%async_computation.56 | async-start | bytes 1048576 | tf_op jit(solution)/shard_map/psum | solution.py:386
  1087.5 316.9 %copy-start.48 = (bf16[128,256]{1,0:T(8,128)(2,1)}, bf16[128,256]{1,0:T(8,128)(2,1)S(1)}, u32[]{:S(2)}) copy-start(bf16[128,256]{1,0:T(8,128)(2,1)S(1)} %subtract_convert_fusion) | copy-start | bytes 196612
  1093.6 352.9 %copy-start.38 = (pred[128,2048]{0,1:T(8,128)(4,1)S(1)}, pred[128,2048]{0,1:T(8,128)(4,1)}, u32[]{:S(2)}) copy-start(pred[128,2048]{0,1:T(8,128)(4,1)} %get-tuple-element.201) | copy-start | bytes 786436
  1227.0 116.4 %all-gather.47.cloned.1.call-start = ((), (), s32[]{:S(2)}) async-start(), calls=%async_computation.18 | async-start | bytes 1114112 | tf_op jit(solution)/shard_map/all_gather | solution.py:81
  1227.8 149.7 %all-gather.45.cloned.1.call-start = ((), (), s32[]{:S(2)}) async-start(), calls=%async_computation.17 | async-start | bytes 1114112 | tf_op jit(solution)/shard_map/all_gather | solution.py:80
  1228.4 183.2 %all-gather.41.cloned.1.call-start = ((), (), s32[]{:S(2)}) async-start(), calls=%async_computation.15 | async-start | bytes 1114112 | tf_op jit(solution)/shard_map/all_gather | solution.py:82
  1230.0 216.4 %copy-start.56 = (f32[128,128]{1,0:T(8,128)}, f32[128,128]{1,0:T(8,128)S(1)}, u32[]{:S(2)}) copy-start(f32[128,128]{1,0:T(8,128)S(1)} %get-tuple-element.166) | copy-start | bytes 196612
  1282.5 163.9 %all-gather.49.cloned.1.call-start = ((), (), s32[]{:S(2)}) async-start(), calls=%async_computation.19 | async-start | bytes 1114112 | tf_op jit(solution)/shard_map/all_gather | solution.py:232
  1405.3 77.3 %all-gather.43.cloned.1.call-start = ((), (), s32[]{:S(2)}) async-start(), calls=%async_computation.16 | async-start | bytes 1114112 | tf_op jit(solution)/shard_map/all_gather | solution.py:233
  1413.9 104.4 %all-gather.51.cloned.1.call-start = ((), (), s32[]{:S(2)}) async-start(), calls=%async_computation.20 | async-start | bytes 1114112 | tf_op jit(solution)/shard_map/all_gather | solution.py:85
  1414.5 195.6 %all-reduce.22.cloned.1.call-start = ((), (), s32[]{:S(2)}) async-start(), calls=%async_computation.21 | async-start | bytes 2097152 | tf_op jit(solution)/shard_map/psum | solution.py:241
  1448.5 772.0 %copy-start.80 = (f32[2,128]{1,0:T(2,128)}, f32[2,128]{1,0:T(2,128)S(1)}, u32[]{:S(2)}) copy-start(f32[2,128]{1,0:T(2,128)S(1)} %log_add_fusion.1) | copy-start | bytes 3076
  1520.9 141.0 %all-gather.53.cloned.1.call-start = ((), (), s32[]{:S(2)}) async-start(), calls=%async_computation.22 | async-start | bytes 8912896 | tf_op jit(solution)/shard_map/all_gather | solution.py:93
  1521.6 194.9 %all-gather.55.cloned.1.call-start = ((), (), s32[]{:S(2)}) async-start(), calls=%async_computation.23 | async-start | bytes 8912896 | tf_op jit(solution)/shard_map/all_gather | solution.py:94
  1522.2 257.8 %all-gather.57.cloned.1.call-start = ((), (), s32[]{:S(2)}) async-start(), calls=%async_computation.24 | async-start | bytes 8912896 | tf_op jit(solution)/shard_map/all_gather | solution.py:95
  1522.9 371.0 %all-reduce.24.cloned.1.call-start = ((), (), s32[]{:S(2)}) async-start(), calls=%async_computation.25 | async-start | bytes 1048576 | tf_op jit(solution)/shard_map/psum | solution.py:279
  1808.9 145.3 %all-gather.77.cloned.1.call-start = ((), (), s32[]{:S(2)}) async-start(), calls=%async_computation.37 | async-start | bytes 8912896 | tf_op jit(solution)/shard_map/all_gather | solution.py:95
  1894.0 113.5 %all-gather.79.cloned.1.call-start = ((), (), s32[]{:S(2)}) async-start(), calls=%async_computation.38 | async-start | bytes 8912896 | tf_op jit(solution)/shard_map/all_gather | solution.py:93
  1894.6 167.9 %all-gather.81.cloned.1.call-start = ((), (), s32[]{:S(2)}) async-start(), calls=%async_computation.39 | async-start | bytes 8912896 | tf_op jit(solution)/shard_map/all_gather | solution.py:94
  1895.3 286.3 %all-reduce.30.cloned.1.call-start = ((), (), s32[]{:S(2)}) async-start(), calls=%async_computation.40 | async-start | bytes 1048576 | tf_op jit(solution)/shard_map/psum | solution.py:316
  2095.0 120.2 %all-gather.83.cloned.1.call-start = ((), (), s32[]{:S(2)}) async-start(), calls=%async_computation.41 | async-start | bytes 1114112 | tf_op jit(solution)/shard_map/all_gather | solution.py:85
  2095.8 189.3 %reduce-scatter.22.cloned.1.call-start = ((), (), s32[]{:S(2)}) async-start(), calls=%async_computation.43 | async-start | bytes 1114112 | tf_op jit(solution)/shard_map/reduce_scatter | solution.py:347
  2186.5 319.5 %copy-start.10 = (f32[128,2048]{1,0:T(8,128)}, f32[128,2048]{1,0:T(8,128)S(1)}, u32[]{:S(2)}) copy-start(f32[128,2048]{1,0:T(8,128)S(1)} %get-tuple-element.135) | copy-start | bytes 3145732
  2223.3 94.8 %all-gather.85.cloned.1.call-start = ((), (), s32[]{:S(2)}) async-start(), calls=%async_computation.42 | async-start | bytes 1114112 | tf_op jit(solution)/shard_map/all_gather | solution.py:80
  2224.1 128.2 %all-gather.87.cloned.1.call-start = ((), (), s32[]{:S(2)}) async-start(), calls=%async_computation.44 | async-start | bytes 1114112 | tf_op jit(solution)/shard_map/all_gather | solution.py:81
  2224.6 162.0 %all-gather.89.cloned.1.call-start = ((), (), s32[]{:S(2)}) async-start(), calls=%async_computation.45 | async-start | bytes 1114112 | tf_op jit(solution)/shard_map/all_gather | solution.py:82
  2225.4 225.3 %reduce-scatter.36.cloned.1.call-start = ((), (), s32[]{:S(2)}) async-start(), calls=%async_computation.62 | async-start | bytes 1114112 | tf_op jit(solution)/shard_map/convert_element_type | solution.py:377
  2230.8 223.3 %copy-start.59 = (s32[256]{0:T(256)S(1)}, s32[256]{0:T(256)}, u32[]{:S(2)}) copy-start(s32[256]{0:T(256)} %copy-done.58) | copy-start | bytes 3076
  2233.2 339.7 %all-reduce.32.cloned.1.call-start = ((), (), s32[]{:S(2)}) async-start(), calls=%async_computation.46 | async-start | bytes 1048576 | tf_op jit(solution)/shard_map/psum | solution.py:386
  2455.2 180.1 %reduce-scatter.42.cloned.1.call-start = ((), (), s32[]{:S(2)}) async-start(), calls=%async_computation.65 | async-start | bytes 8912896
  2505.9 193.4 %reduce-scatter.40.cloned.1.call-start = ((), (), s32[]{:S(2)}) async-start(), calls=%async_computation.64 | async-start | bytes 1114112
  2509.2 252.8 %reduce-scatter.26.cloned.1.call-start = ((), (), s32[]{:S(2)}) async-start(), calls=%async_computation.57 | async-start | bytes 1114112 | tf_op jit(solution)/shard_map/reduce_scatter | solution.py:104
  2513.1 311.1 %reduce-scatter.28.cloned.1.call-start = ((), (), s32[]{:S(2)}) async-start(), calls=%async_computation.58 | async-start | bytes 1114112 | tf_op jit(solution)/shard_map/reduce_scatter | solution.py:107
  2516.2 370.5 %reduce-scatter.30.cloned.1.call-start = ((), (), s32[]{:S(2)}) async-start(), calls=%async_computation.59 | async-start | bytes 1114112 | tf_op jit(solution)/shard_map/reduce_scatter | solution.py:110
  2518.4 443.9 %reduce-scatter.32.cloned.1.call-start = ((), (), s32[]{:S(2)}) async-start(), calls=%async_computation.60 | async-start | bytes 8912896 | tf_op jit(solution)/shard_map/reduce_scatter | solution.py:125
  2541.7 496.2 %reduce-scatter.34.cloned.1.call-start = ((), (), s32[]{:S(2)}) async-start(), calls=%async_computation.61 | async-start | bytes 8912896 | tf_op jit(solution)/shard_map/reduce_scatter | solution.py:128
  2585.9 23.7 all-to-all-start.3
  2609.6 126.9 %all-to-all-start.1 = ((bf16[2,128,2048]{2,0,1:T(2,128)(2,1)}), bf16[2,128,2048]{2,0,1:T(2,128)(2,1)}, u32[]{:S(2)}, u32[]{:S(2)}) async-start(bf16[2,128,2048]{2,0,1:T(2,128)(2,1)} %get-tuple-element.172), calls=%async_computation.1 | async-start | bytes 2097152 | tf_op jit(solution)/shard_map/all_to_all | solution.py:411
  2736.5 303.4 %copy-start.1 = (bf16[2,128,2048]{2,1,0:T(8,128)(2,1)S(1)}, bf16[2,128,2048]{2,1,0:T(8,128)(2,1)}, u32[]{:S(2)}) copy-start(bf16[2,128,2048]{2,1,0:T(8,128)(2,1)} %param.20) | copy-start | bytes 3145732
  (104 other events, 6340.6 us)
Sparse Core Ops, SparseCore 0:
  11.4 7.6 sort.54.cloned.1.call-done
  67.7 2.3 sort.56.cloned.1.call-done
  86.0 32.0 all-gather.62
  119.7 32.5 all-gather.64
  153.9 32.4 all-gather.58
  188.6 32.5 all-gather.66
  223.5 34.0 all-gather.60
  259.3 34.1 all-gather.68
  296.7 88.6 all-reduce.25
  387.0 50.0 all-gather.70
  438.9 53.1 all-gather.72
  493.6 61.7 all-gather.74
  584.4 84.9 all-reduce.27
  670.8 58.6 all-gather.90
  731.0 51.6 all-gather.92
  784.2 53.1 all-gather.94
  870.3 86.4 all-reduce.33
  958.3 31.9 all-gather.96
  997.5 61.5 reduce-scatter.23
  1060.7 31.1 all-gather.98
  1093.6 32.5 all-gather.100
  1127.9 32.4 all-gather.102
  1162.8 61.6 reduce-scatter.37
  1227.5 83.6 all-reduce.35
  1312.9 30.4 all-gather.46
  1344.9 32.4 all-gather.44
  1379.0 32.4 all-gather.40
  1413.8 32.5 all-gather.48
  1448.6 34.0 all-gather.42
  1484.1 34.1 all-gather.50
  1521.4 88.6 all-reduce.21
  1611.7 50.0 all-gather.52
  1663.4 53.1 all-gather.54
  1718.2 61.7 all-gather.56
  1809.0 84.9 all-reduce.23
  1895.5 58.6 all-gather.76
  1955.8 51.6 all-gather.78
  2009.3 53.1 all-gather.80
  2095.2 86.3 all-reduce.29
  2183.2 31.9 all-gather.82
  2223.4 61.5 reduce-scatter.21
  2286.9 31.1 all-gather.84
  2319.8 32.4 all-gather.86
  2354.1 32.4 all-gather.88
  2389.0 61.6 reduce-scatter.35
  2453.6 83.6 all-reduce.31
  2540.0 2.3 sort.58.cloned.1.call-done
  2545.0 90.3 reduce-scatter.41
  2638.1 61.1 reduce-scatter.39
  2701.8 60.1 reduce-scatter.25
  2764.2 59.9 reduce-scatter.27
  2826.7 59.9 reduce-scatter.29
  2888.9 73.3 reduce-scatter.31
  2964.6 73.1 reduce-scatter.33
  (3 shorter events, 0.0 us)
where the time goes:
time: 3060 us; the launch traced here: 3050 us
  waiting for transfers between devices  2140 us (70%)
  blocking collectives  283 us (9%)
  matrix products  241 us (8%)
  local copies, waits for them, and re-layouts  208 us (7%)
  other arithmetic  126 us (4%)
    all_gather x4, waiting for transfers between devices, fetch_experts(): lax.all_gather(tied[3], 'dp', axis=2, tiled=True)  214 us
    all_gather x4, waiting for transfers between devices, fetch_experts(): lax.all_gather(tied[2], 'dp', axis=1, tiled=True)  185 us
    all_gather x4, waiting for transfers between devices, fetch_experts(): lax.all_gather(tied[1], 'dp', axis=1, tiled=True)  173 us
    psum x2, waiting for transfers between devices, body(): lax.psum(moe_grad_part.astype(jnp.bfloat16), 'tensor').astype(jnp.float32)  172 us
    psum x2, waiting for transfers between devices, body(): lax.psum(moe_part.astype(jnp.bfloat16), 'tensor').astype(jnp.float32)  170 us
    convert_element_type x2, waiting for transfers between devices, body(): delta_value.reshape(row_count, local_width).astype(jnp.bfloat16)  128 us
    all_gather x4, waiting for transfers between devices, fetch_attention(): lax.all_gather(tied[6], 'dp', axis=1, tiled=True)  125 us
    psum x2, waiting for transfers between devices, body(): lax.psum(jnp.dot(mixed_b, out_full, preferred_element_type=jnp.float32),...  108 us
  transfers between devices with their start and end apart: 54, of which 50 were waited for; matrix products, arithmetic and copies ran while one was open for 13% of the time, Pallas kernels for 0%

commit v1 on v0

v1 whole, which is shorter than its diff:
```python
import jax
import jax.numpy as jnp
from jax import lax
from jax.experimental import pallas as pl
from jax.experimental.pallas import tpu as pltpu
from jax.sharding import PartitionSpec as P

HEAD = 128
MIB = 1024 * 1024
bf16 = jnp.bfloat16
f32 = jnp.float32

epsilon = 1e-05
rope_base = 10000.0


def rope_tables(position):
    half_dim = HEAD // 2
    frequency = rope_base ** (-(jnp.arange(half_dim, dtype=f32) * 2.0 / HEAD))
    angle = position[:, None] * frequency[None, :]
    cosine = jnp.concatenate([jnp.cos(angle), jnp.cos(angle)], axis=-1)
    sine = jnp.concatenate([jnp.sin(angle), jnp.sin(angle)], axis=-1)
    return (cosine[:, None, :], sine[:, None, :])


def rotate(values, cosine, sine):
    half_dim = values.shape[-1] // 2
    turned = jnp.concatenate([-values[..., half_dim:], values[..., :half_dim]], axis=-1)
    return values * cosine + turned * sine


def rotate_back(gradient, cosine, sine):
    half_dim = gradient.shape[-1] // 2
    scaled = gradient * sine
    turned = jnp.concatenate([scaled[..., half_dim:], -scaled[..., :half_dim]], axis=-1)
    return gradient * cosine + turned


def norm_factor(values):
    return lax.rsqrt(jnp.mean(values * values, axis=-1, keepdims=True) + epsilon)


def norm_back(values, factor, gain, gradient):
    gained = gradient * gain
    inner_sum = jnp.sum(gained * values, axis=-1, keepdims=True)
    return factor * gained - values * (factor * factor * factor) * inner_sum / values.shape[-1]


def dot_nn(left_side, right_side):
    return jnp.dot(left_side, right_side, preferred_element_type=f32)


def dot_tn(left_side, right_side):
    return lax.dot_general(
        left_side, right_side, (((0,), (0,)), ((), ())), preferred_element_type=f32
    )


def dot_nt(left_side, right_side):
    return lax.dot_general(
        left_side, right_side, (((1,), (1,)), ((), ())), preferred_element_type=f32
    )


def exchange(value, axis):
    return lax.all_to_all(value, axis, split_axis=0, concat_axis=0, tiled=True)


def spread(value, axis):
    count = lax.axis_size(axis)
    return exchange(jnp.broadcast_to(value[None], (count,) + value.shape), axis)


BLOCK = 256

KEYS = slice(0, 128)
VALUES = slice(128, 256)
QUERIES = slice(256, 288)
Q_BLOCKS = 4


def masked_scores(query, keys, key_place, query_place, query_start):
    scores = dot_nt(query, keys) * (HEAD ** (-0.5))
    visible = (key_place <= query_place) & (key_place >= query_start)
    return jnp.where(visible, scores, -1e30)


def attention_kernel(packed, key_place, query_place, query_start, mixed, log_total):
    sources = packed.shape[0]
    keys = packed[:, KEYS, :].reshape(sources * 128, HEAD)
    values = packed[:, VALUES, :].reshape(sources * 128, HEAD)
    for part in range(sources // Q_BLOCKS):
        blocks = slice(part * Q_BLOCKS, (part + 1) * Q_BLOCKS)
        rows = slice(part * Q_BLOCKS * 32, (part + 1) * Q_BLOCKS * 32)
        query = packed[blocks, QUERIES, :].reshape(Q_BLOCKS * 32, HEAD)
        scores = masked_scores(
            query, keys, key_place[...], query_place[rows, :], query_start[rows, :]
        )
        peak = jnp.max(scores, axis=-1, keepdims=True)
        weights = jnp.exp(scores - peak)
        total = jnp.sum(weights, axis=-1, keepdims=True)
        probs = (weights / total).astype(bf16)
        mixed[blocks, :, :] = (
            dot_nn(probs, values).astype(bf16).reshape(Q_BLOCKS, 32, HEAD)
        )
        log_total[rows, :] = peak + jnp.log(total)


def attention_back_kernel(
    packed, key_place, query_place, query_start, log_total, delta_mixed, out, key_sum, value_sum
):
    sources = packed.shape[0]
    keys = packed[:, KEYS, :].reshape(sources * 128, HEAD)
    values = packed[:, VALUES, :].reshape(sources * 128, HEAD)
    scale = HEAD ** (-0.5)
    for part in range(sources // Q_BLOCKS):
        blocks = slice(part * Q_BLOCKS, (part + 1) * Q_BLOCKS)
        rows = slice(part * Q_BLOCKS * 32, (part + 1) * Q_BLOCKS * 32)
        query = packed[blocks, QUERIES, :].reshape(Q_BLOCKS * 32, HEAD)
        delta = delta_mixed[blocks, :, :].reshape(Q_BLOCKS * 32, HEAD)
        scores = masked_scores(
            query, keys, key_place[...], query_place[rows, :], query_start[rows, :]
        )
        probs = jnp.exp(scores - log_total[rows, :])
        delta_probs = dot_nt(delta, values)
        inner = jnp.sum(probs * delta_probs, axis=-1, keepdims=True)
        delta_scores = (probs * (delta_probs - inner)).astype(bf16)
        out[blocks, QUERIES, :] = (
            (dot_nn(delta_scores, keys) * scale).astype(bf16).reshape(Q_BLOCKS, 32, HEAD)
        )
        key_term = dot_tn(delta_scores, query)
        value_term = dot_tn(probs.astype(bf16), delta)
        if part == 0:
            key_sum[...] = key_term
            value_sum[...] = value_term
        else:
            key_sum[...] += key_term
            value_sum[...] += value_term
    out[:, KEYS, :] = (key_sum[...] * scale).astype(bf16).reshape(sources, 128, HEAD)
    out[:, VALUES, :] = value_sum[...].astype(bf16).reshape(sources, 128, HEAD)


def attention(packed, key_place, query_place, query_start):
    sources = packed.shape[0]
    return pl.pallas_call(
        attention_kernel,
        out_shape=(
            jax.ShapeDtypeStruct((sources, 32, HEAD), bf16),
            jax.ShapeDtypeStruct((sources * 32, 1), f32),
        ),
        compiler_params=pltpu.CompilerParams(vmem_limit_bytes=40 * MIB),
        name="attention",
    )(packed, key_place, query_place, query_start)


def attention_back(packed, key_place, query_place, query_start, log_total, delta_mixed):
    sources = packed.shape[0]
    return pl.pallas_call(
        attention_back_kernel,
        out_shape=jax.ShapeDtypeStruct(packed.shape, bf16),
        scratch_shapes=[
            pltpu.VMEM((sources * 128, HEAD), f32),
            pltpu.VMEM((sources * 128, HEAD), f32),
        ],
        compiler_params=pltpu.CompilerParams(vmem_limit_bytes=40 * MIB),
        name="attention_back",
    )(packed, key_place, query_place, query_start, log_total, delta_mixed)


def stack_attention_kernel(w_query, w_key, w_value, w_out, out):
    local = w_query.shape[1]
    out[:, :local] = w_query[...]
    out[:, local : 2 * local] = w_key[...]
    out[:, 2 * local : 3 * local] = w_value[...]
    out[:, 3 * local :] = w_out[...].T


def stack_attention(w_query, w_key, w_value, w_out):
    rows, local = w_query.shape
    return pl.pallas_call(
        stack_attention_kernel,
        out_shape=jax.ShapeDtypeStruct((rows, 4 * local), bf16),
        name="stack_attention",
    )(w_query, w_key, w_value, w_out)


def stack_experts_kernel(w_gate, w_up, w_down, out):
    for expert in range(w_gate.shape[0]):
        for index, stored in enumerate((w_gate, w_up, w_down)):
            start = (expert // 2) * 3 * BLOCK + index * BLOCK + (expert % 2) * HEAD
            value = stored[expert]
            out[:, start : start + HEAD] = value.T if stored is w_down else value


def stack_experts(w_gate, w_up, w_down):
    count, rows, hidden = w_gate.shape
    return pl.pallas_call(
        stack_experts_kernel,
        out_shape=jax.ShapeDtypeStruct((rows, 3 * count * hidden), bf16),
        compiler_params=pltpu.CompilerParams(vmem_limit_bytes=24 * MIB),
        name="stack_experts",
    )(w_gate, w_up, w_down)


def experts_kernel(
    rows, rows_t, upstream, upstream_t, gates, weights, out, delta_in, grads, out_sum, delta_sum
):
    step = pl.program_id(0)
    gate_w = weights[:, 0:BLOCK]
    up_w = weights[:, BLOCK : 2 * BLOCK]
    down_w = weights[:, 2 * BLOCK : 3 * BLOCK]
    gate_h = dot_nn(rows[...], gate_w)
    up_h = dot_nn(rows[...], up_w)
    delta_hidden = dot_nn(upstream[...], down_w)
    lane = lax.broadcasted_iota(jnp.int32, gates.shape, 1)
    shares = [
        jnp.sum(jnp.where(lane == step * (BLOCK // 128) + e, gates[...], 0.0), axis=1, keepdims=True)
        for e in range(BLOCK // 128)
    ]
    share = jnp.concatenate([jnp.broadcast_to(s, (s.shape[0], 128)) for s in shares], axis=1)
    sigmoid_gate = 1.0 / (1.0 + jnp.exp(-gate_h))
    active = gate_h * sigmoid_gate
    hidden = (active * up_h * share).astype(bf16)
    delta_hidden = delta_hidden * share
    delta_gate = (
        delta_hidden * up_h * sigmoid_gate * (1.0 + gate_h * (1.0 - sigmoid_gate))
    ).astype(bf16)
    delta_up = (delta_hidden * active).astype(bf16)
    grads[:, 0:BLOCK] = dot_nn(rows_t[...], delta_gate).astype(bf16)
    grads[:, BLOCK : 2 * BLOCK] = dot_nn(rows_t[...], delta_up).astype(bf16)
    grads[:, 2 * BLOCK : 3 * BLOCK] = dot_nn(upstream_t[...], hidden).astype(bf16)
    out_term = dot_nt(hidden, down_w)
    delta_term = dot_nt(delta_gate, gate_w) + dot_nt(delta_up, up_w)

    @pl.when(step == 0)
    def _():
        out_sum[...] = out_term
        delta_sum[...] = delta_term

    @pl.when(step > 0)
    def _():
        out_sum[...] += out_term
        delta_sum[...] += delta_term

    @pl.when(step == pl.num_programs(0) - 1)
    def _():
        out[...] = out_sum[...].astype(bf16)
        delta_in[...] = delta_sum[...].astype(bf16)


def experts(rows, rows_t, upstream, upstream_t, gates, weights):
    count, width = rows.shape
    steps = weights.shape[1] // (3 * BLOCK)

    def whole(shape):
        return pl.BlockSpec(shape, lambda c: (0, 0))

    return pl.pallas_call(
        experts_kernel,
        grid=(steps,),
        in_specs=[
            whole((count, width)),
            whole((width, count)),
            whole((count, width)),
            whole((width, count)),
            whole(gates.shape),
            pl.BlockSpec((width, 3 * BLOCK), lambda c: (0, c)),
        ],
        out_specs=[
            whole((count, width)),
            whole((count, width)),
            pl.BlockSpec((width, 3 * BLOCK), lambda c: (0, c)),
        ],
        out_shape=(
            jax.ShapeDtypeStruct((count, width), bf16),
            jax.ShapeDtypeStruct((count, width), bf16),
            jax.ShapeDtypeStruct(weights.shape, bf16),
        ),
        scratch_shapes=[pltpu.VMEM((count, width), f32), pltpu.VMEM((count, width), f32)],
        compiler_params=pltpu.CompilerParams(
            dimension_semantics=("arbitrary",), vmem_limit_bytes=56 * MIB
        ),
        name="experts",
    )(rows, rows_t, upstream, upstream_t, gates, weights)


def body(
    tokens,
    cotangent,
    pack_perm,
    lengths,
    routes,
    gates,
    attn_gain,
    w_query,
    w_key,
    w_value,
    query_gain,
    key_gain,
    w_out,
    moe_gain,
    w_gate,
    w_up,
    w_down,
):
    dp = lax.axis_size("dp")
    te = lax.axis_size("tensor")
    me = lax.axis_index("dp")
    my_te = lax.axis_index("tensor")
    micro, block, width = tokens.shape
    ranks = block // dp
    own = micro * block
    part = own // te
    local = w_query.shape[1]
    heads = local // HEAD
    head_part = HEAD // dp
    quarters = dp // (micro * heads)
    expert_count = w_gate.shape[0]

    attn_local = stack_attention(w_query, w_key, w_value, w_out)
    attn_w = lax.all_gather(attn_local, "dp", axis=0, tiled=True)
    moe_local = stack_experts(w_gate, w_up, w_down)

    blocks = pack_perm.reshape(micro, dp, block)
    root = blocks // block
    earlier = jnp.arange(block)[None, :] < jnp.arange(block)[:, None]
    rank = jnp.sum(
        ((root[:, :, :, None] == root[:, :, None, :]) & earlier).astype(jnp.int32), axis=3
    )
    from_me = (root == me)[:, :, None, :] & (
        rank[:, :, None, :] == jnp.arange(ranks, dtype=jnp.int32)[None, None, :, None]
    )
    given = jnp.sum(jnp.where(from_me, (blocks - me * block)[:, :, None, :], 0), axis=3)
    given = given + (jnp.arange(micro, dtype=jnp.int32) * block)[:, None, None]
    row_index = jnp.arange(own, dtype=jnp.int32)
    send_order = lax.dynamic_index_in_dim(given, my_te, axis=2, keepdims=False).T.reshape(part)
    home_order = given.transpose(2, 1, 0).reshape(own)
    send_hot = (send_order[:, None] == row_index[None, :]).astype(bf16)
    home_hot = (row_index[:, None] == home_order[None, :]).astype(bf16)
    slot = rank * dp + root
    slot_hot = slot[:, :, None, :] == jnp.arange(block, dtype=jnp.int32)[None, None, :, None]
    place_in = jnp.sum(
        jnp.where(slot_hot, jnp.arange(block, dtype=jnp.int32)[None, None, None, :], 0), axis=3
    )
    place_of = place_in + (jnp.arange(dp, dtype=jnp.int32) * block)[None, :, None]

    def chosen(values):
        return dot_nn(send_hot, values.reshape(own, width)).astype(bf16).reshape(dp, micro, width)

    gains = jnp.stack(
        [
            attn_gain,
            moe_gain,
            jnp.concatenate(
                [
                    query_gain.reshape(-1),
                    key_gain.reshape(-1),
                    jnp.zeros((block - 2 * heads * head_part,), bf16),
                ]
            ),
            jnp.zeros((block,), bf16),
        ]
    )
    dealt = jnp.concatenate(
        [
            jnp.concatenate([chosen(tokens), chosen(cotangent)], axis=1),
            jnp.broadcast_to(gains[None], (dp,) + gains.shape),
        ],
        axis=2,
    )
    dealt = exchange(dealt, "dp")
    part_tokens = dealt[:, :micro, :width].reshape(part, width)
    part_cotangent = dealt[:, micro:, :width].reshape(part, width)
    attn_gain_f = dealt[:, 0, width:].reshape(width).astype(f32)
    moe_gain_f = dealt[:, 1, width:].reshape(width).astype(f32)

    def head_gain(cut):
        return cut.reshape(dp, heads, head_part).transpose(1, 0, 2).reshape(local).astype(f32)

    query_scale = head_gain(dealt[:, 2, width : width + heads * head_part])
    key_scale = head_gain(
        dealt[:, 2, width + heads * head_part : width + 2 * heads * head_part]
    )
    own_tokens = spread(part_tokens, "tensor").reshape(own, width)

    moe_local = lax.optimization_barrier((moe_local, part_tokens))[0]
    moe_w = lax.all_gather(moe_local, "dp", axis=0, tiled=True)

    seq_ends = jnp.cumsum(lengths, axis=1)
    seq_starts = seq_ends - lengths

    def start_of(place, ends, starts):
        inside = (place[..., None] >= starts) & (place[..., None] < ends)
        return jnp.sum(jnp.where(inside, starts, 0), axis=-1)

    own_place = lax.dynamic_index_in_dim(place_of, me, axis=1, keepdims=False)
    own_start = start_of(own_place, seq_ends[:, None, :], seq_starts[:, None, :])
    position = (own_place - own_start).astype(f32)
    position = position.reshape(micro, ranks, dp).transpose(1, 2, 0).reshape(own)
    cosine, sine = rope_tables(position)
    pair_micro = me // (heads * quarters)
    quarter = me % quarters
    key_place = lax.dynamic_index_in_dim(place_of, pair_micro, axis=0, keepdims=False)
    query_place = lax.dynamic_slice_in_dim(
        key_place, quarter * (block // quarters), block // quarters, axis=1
    ).reshape(-1, 1)
    pair_ends = lax.dynamic_index_in_dim(seq_ends, pair_micro, axis=0)
    pair_starts = lax.dynamic_index_in_dim(seq_starts, pair_micro, axis=0)
    query_start = start_of(query_place, pair_ends[None], pair_starts[None])
    key_place = key_place.reshape(1, -1)

    hot = routes[..., None] == jnp.arange(expert_count, dtype=jnp.int32)
    dense = jnp.sum(jnp.where(hot, gates[..., None], 0.0), axis=2)
    own_slot_hot = lax.dynamic_index_in_dim(slot_hot, me, axis=1, keepdims=False)
    share = jnp.einsum(
        "msj,mje->mse", own_slot_hot.astype(f32), dense, precision=lax.Precision.HIGHEST
    )
    share = share.reshape(micro, ranks, dp, expert_count).transpose(1, 2, 0, 3)
    share = share.reshape(own, expert_count)
    share = jnp.pad(share, ((0, 0), (0, HEAD - expert_count)))

    qkv_w = attn_w[:, : 3 * local]
    out_w = attn_w[:, 3 * local : 4 * local]
    inputs = own_tokens.astype(f32)
    attn_factor = norm_factor(inputs)
    normed_b = (inputs * attn_factor * attn_gain_f).astype(bf16)
    qkv = dot_nn(normed_b, qkv_w)
    query_pre = qkv[:, :local]
    key_pre = qkv[:, local : 2 * local]
    value_b = qkv[:, 2 * local :].astype(bf16)
    squares = jnp.stack(
        [jnp.sum(query_pre * query_pre, axis=1), jnp.sum(key_pre * key_pre, axis=1)]
    )
    squares = jnp.sum(spread(squares, "tensor"), axis=0)
    factors = lax.rsqrt(squares / width + epsilon)
    query_factor = factors[0][:, None]
    key_factor = factors[1][:, None]
    query_b = rotate(
        (query_pre * query_factor * query_scale).reshape(own, heads, HEAD), cosine, sine
    ).astype(bf16)
    key_b = rotate(
        (key_pre * key_factor * key_scale).reshape(own, heads, HEAD), cosine, sine
    ).astype(bf16)

    def to_pairs(values):
        cut = values.reshape(ranks, dp, micro, heads, HEAD)
        return cut.transpose(2, 3, 0, 1, 4).reshape(micro, heads, block, HEAD)

    def to_quarters(values):
        return to_pairs(values).reshape(micro, heads, quarters, block // quarters, HEAD)

    def from_pairs(values):
        cut = values.reshape(micro, heads, ranks, dp, HEAD)
        return cut.transpose(2, 3, 0, 1, 4).reshape(own, local)

    copies = (micro, heads, quarters, block, HEAD)
    sent = jnp.concatenate(
        [
            jnp.broadcast_to(to_pairs(key_b)[:, :, None], copies),
            jnp.broadcast_to(to_pairs(value_b.reshape(own, heads, HEAD))[:, :, None], copies),
            to_quarters(query_b),
        ],
        axis=3,
    )
    packed = exchange(sent.reshape(dp, 2 * block + block // quarters, HEAD), "dp")
    pair_mixed, log_total = attention(packed, key_place, query_place, query_start)
    mixed_b = from_pairs(exchange(pair_mixed, "dp"))

    def shared_sum(value):
        got = exchange(value.astype(bf16).reshape(te, part, width), "tensor")
        return jnp.sum(got.astype(f32), axis=0)

    part_inputs = part_tokens.astype(f32)
    part_upstream = part_cotangent.astype(f32)
    hidden_one = part_inputs + shared_sum(dot_nt(mixed_b, out_w))

    moe_factor = norm_factor(hidden_one)
    moe_in = spread((hidden_one * moe_factor * moe_gain_f).astype(bf16), "tensor")
    moe_in = moe_in.reshape(own, width)
    own_cotangent = spread(part_cotangent, "tensor").reshape(own, width)
    moe_part, moe_grad_part, moe_grads = experts(
        moe_in, moe_in.T, own_cotangent, own_cotangent.T, share, moe_w
    )
    moe_grads = lax.psum_scatter(moe_grads, "dp", scatter_dimension=0, tiled=True)
    moe_grad = shared_sum(moe_grad_part)
    grad_moe_gain = jnp.sum(moe_grad * hidden_one * moe_factor, axis=0)
    delta_one = part_upstream + norm_back(hidden_one, moe_factor, moe_gain_f, moe_grad)
    delta_attn = spread(delta_one.astype(bf16), "tensor").reshape(own, width)
    grad_out = dot_tn(delta_attn, mixed_b)
    delta_mixed = dot_nn(delta_attn, out_w).astype(bf16)
    pair_delta = exchange(
        to_quarters(delta_mixed.reshape(own, heads, HEAD)).reshape(dp, block // quarters, HEAD),
        "dp",
    )
    pair_grads = attention_back(
        packed, key_place, query_place, query_start, log_total, pair_delta
    )
    got = exchange(pair_grads, "dp").reshape(micro, heads, quarters, -1, HEAD)
    delta_key = from_pairs(jnp.sum(got[:, :, :, KEYS].astype(f32), axis=2))
    delta_value = from_pairs(jnp.sum(got[:, :, :, VALUES].astype(f32), axis=2))
    delta_query = from_pairs(got[:, :, :, QUERIES].astype(f32))
    delta_qnorm = rotate_back(delta_query.reshape(own, heads, HEAD), cosine, sine)
    delta_qnorm = delta_qnorm.reshape(own, local)
    delta_knorm = rotate_back(delta_key.reshape(own, heads, HEAD), cosine, sine)
    delta_knorm = delta_knorm.reshape(own, local)
    grad_qgain = jnp.sum(delta_qnorm * query_pre * query_factor, axis=0)
    grad_kgain = jnp.sum(delta_knorm * key_pre * key_factor, axis=0)
    weighted_query = delta_qnorm * query_scale
    weighted_key = delta_knorm * key_scale
    inner = jnp.stack(
        [jnp.sum(weighted_query * query_pre, axis=1), jnp.sum(weighted_key * key_pre, axis=1)]
    )
    inner = jnp.sum(spread(inner, "tensor"), axis=0) / width
    delta_qpre = query_factor * weighted_query - query_pre * (
        query_factor * query_factor * query_factor
    ) * inner[0][:, None]
    delta_kpre = key_factor * weighted_key - key_pre * (
        key_factor * key_factor * key_factor
    ) * inner[1][:, None]
    delta_pre = jnp.concatenate(
        [delta_qpre.astype(bf16), delta_kpre.astype(bf16), delta_value.astype(bf16)], axis=1
    )
    attn_grad = dot_nt(delta_pre, qkv_w)
    grad_qkv = dot_tn(normed_b, delta_pre)

    def gain_cut(gradient):
        return gradient.reshape(heads, dp, head_part).transpose(1, 0, 2).reshape(dp, -1)

    below = jnp.concatenate([gain_cut(grad_qgain), gain_cut(grad_kgain)], axis=1)
    below = jnp.pad(below[:, None], ((0, 0), (0, 15), (0, 4 * local - below.shape[1])))
    attn_grads = jnp.concatenate(
        [
            jnp.concatenate([grad_qkv, grad_out], axis=1).astype(bf16).reshape(dp, block, -1),
            below.astype(bf16),
        ],
        axis=1,
    )
    grad_attn_gain = jnp.sum(attn_grad * inputs * attn_factor, axis=0)
    mine = (jnp.arange(te) == my_te)[:, None, None]

    def with_part(terms, rows):
        terms = terms.astype(f32).reshape(te, part, width)
        return (terms + jnp.where(mine, rows[None], 0.0)).astype(bf16)

    out_terms = with_part(moe_part, hidden_one)
    grad_terms = with_part(norm_back(inputs, attn_factor, attn_gain_f, attn_grad), delta_one)

    def gain_lanes(gradient):
        return gradient.reshape(dp, te, block // te).transpose(1, 0, 2)

    lanes = jnp.concatenate([gain_lanes(grad_attn_gain), gain_lanes(grad_moe_gain)], axis=2)
    lanes = jnp.pad(
        lanes.astype(bf16)[:, :, None],
        ((0, 0), (0, 0), (0, 2 * micro - 1), (0, block - lanes.shape[2])),
    )
    home = jnp.concatenate(
        [
            jnp.concatenate(
                [
                    out_terms.reshape(te, dp, micro, width),
                    grad_terms.reshape(te, dp, micro, width),
                ],
                axis=2,
            ),
            lanes,
        ],
        axis=3,
    )
    home = exchange(home.reshape(te * dp, 2 * micro, width + block), ("tensor", "dp"))
    attn_grads = lax.optimization_barrier((attn_grads, moe_grads, home))[0]
    attn_grads = lax.psum_scatter(attn_grads, "dp", scatter_dimension=0, tiled=True)[0]
    attn_grads = attn_grads.astype(f32)
    home = jnp.sum(home.reshape(te, dp, 2 * micro, width + block).astype(f32), axis=0)
    gain_sum = jnp.sum(home[:, :, width:], axis=0, keepdims=True)
    home = jnp.concatenate(
        [home[:, :, :width], jnp.broadcast_to(gain_sum, (dp,) + gain_sum.shape[1:])], axis=2
    ).astype(bf16)
    home = spread(home, "tensor")
    gain_sum = home[:, 0, 0, width:].astype(f32)
    out_rows = home[:, :, :micro, :width].reshape(own, width)
    grad_rows = home[:, :, micro:, :width].reshape(own, width)
    output = dot_nn(home_hot, out_rows).astype(bf16).reshape(micro, block, width)
    input_grad = dot_nn(home_hot, grad_rows).astype(bf16).reshape(micro, block, width)

    gain_part = block // te
    head_cut = heads * head_part
    expert_grads = moe_grads.reshape(block, expert_count // 2, 3, 2, HEAD)
    expert_grads = expert_grads.transpose(2, 1, 3, 0, 4)
    expert_grads = expert_grads.reshape(3, expert_count, block, HEAD).astype(f32)
    return (
        output,
        input_grad,
        gain_sum[:, :gain_part].reshape(block),
        attn_grads[:block, :local],
        attn_grads[:block, local : 2 * local],
        attn_grads[:block, 2 * local : 3 * local],
        attn_grads[block, :head_cut].reshape(heads, head_part),
        attn_grads[block, head_cut : 2 * head_cut].reshape(heads, head_part),
        attn_grads[:block, 3 * local :].T,
        gain_sum[:, gain_part : 2 * gain_part].reshape(block),
        expert_grads[0],
        expert_grads[1],
        expert_grads[2].transpose(0, 2, 1),
    )


def solution(mesh):
    placed = (
        P(None, "dp", None),
        P(None, "dp", None),
        P(),
        P(),
        P(None, "dp", None),
        P(None, "dp", None),
        P("dp"),
        P("dp", "tensor"),
        P("dp", "tensor"),
        P("dp", "tensor"),
        P("tensor", "dp"),
        P("tensor", "dp"),
        P("tensor", "dp"),
        P("dp"),
        P(None, "dp", "tensor"),
        P(None, "dp", "tensor"),
        P(None, "tensor", "dp"),
    )
    return jax.shard_map(
        body,
        mesh=mesh,
        in_specs=placed,
        out_specs=(
            P(None, "dp", None),
            P(None, "dp", None),
            P("dp"),
            P("dp", "tensor"),
            P("dp", "tensor"),
            P("dp", "tensor"),
            P("tensor", "dp"),
            P("tensor", "dp"),
            P("tensor", "dp"),
            P("dp"),
            P(None, "dp", "tensor"),
            P(None, "dp", "tensor"),
            P(None, "tensor", "dp"),
        ),
        check_vma=False,
    )
```

time: 3060 us -> 585 us (0.19)
  waiting for transfers between devices: 2140 us -> 273 us
  blocking collectives: 283 us -> 11 us
  matrix products: 241 us -> 21.3 us
  local copies, waits for them, and re-layouts: 208 us -> 77 us
  other arithmetic: 126 us -> 55.8 us
  Pallas kernels: 0 us -> 47.5 us
  starting transfers between devices: 26.5 us -> 72.1 us
    all_gather x32 -> x2, waiting for transfers between devices: 1040 us -> 32.3 us  [the longest x1 32.3 us: body(): moe_w = lax.all_gather(moe_local, 'dp', axis=0, tiled=True)]
    psum x8 -> x0, waiting for transfers between devices: 478 us -> none  [the longest x2 172 us: body(): lax.psum(moe_grad_part.astype(jnp.bfloat16), 'tensor').astype(jnp.float32)]
    reduce_scatter x7 -> x2, waiting for transfers between devices: 380 us -> 42.2 us  [the longest x1 27.2 us: body(): lax.psum_scatter(attn_grads, 'dp', scatter_dimension=0, tiled=True)[0]]
    dot_general x54 -> x11, matrix products: 241 us -> 21.3 us  [the longest x6 8.74 us: dot_nn(): return jnp.dot(left_side, right_side, preferred_element_type=f32)]
    all_to_all x3 -> x14, waiting for transfers between devices: 20.4 us -> 199 us  [exchange(): return lax.all_to_all(value, axis, split_axis=0, concat_axis=0, tiled=True)]
    all_gather x8 -> x0, blocking collectives: 137 us -> none  [the longest x2 35.8 us: fetch_experts(): lax.all_gather(tied[0], 'dp', axis=0, tiled=True)]
    convert_element_type x2 -> x0, waiting for transfers between devices: 128 us -> none  [body(): delta_value.reshape(row_count, local_width).astype(jnp.bfloat16)]
    gather x19 -> x0, local copies, waits for them, and re-layouts: 117 us -> none  [the longest x2 25.9 us: body(): expert_out[target].reshape(row_count, top_count, model_width)]
  transfers between devices with their start and end apart: 54 -> 18, of which waited for: 50 -> 17; matrix products, arithmetic and copies ran while one was open for 13% -> 25% of each run, Pallas kernels for 0% -> 2%
where the time goes in v1:
time: 585 us; the launch traced here: 573 us
  waiting for transfers between devices  273 us (47%)
  local copies, waits for them, and re-layouts  77 us (13%)
  starting transfers between devices  72.1 us (12%)
  other arithmetic  55.8 us (10%)
  Pallas kernels  47.5 us (8%)
  matrix products  21.3 us (4%)
  between operations  15.2 us (3%)
  blocking collectives  11 us (2%)
    all_to_all x14, waiting for transfers between devices, exchange(): return lax.all_to_all(value, axis, split_axis=0, concat_axis=0, tiled=True)  199 us
    all_to_all x14, starting transfers between devices, exchange(): return lax.all_to_all(value, axis, split_axis=0, concat_axis=0, tiled=True)  71.9 us
    pallas_call x1, Pallas kernels, experts(): pl.pallas_call(experts_kernel, grid=(steps,), in_specs=[whole((count, wid...  35.7 us
    all_gather x1, waiting for transfers between devices, body(): moe_w = lax.all_gather(moe_local, 'dp', axis=0, tiled=True)  32.3 us
    reduce_scatter x1, waiting for transfers between devices, body(): lax.psum_scatter(attn_grads, 'dp', scatter_dimension=0, tiled=True)[0]  27.2 us
    reduce_scatter x1, waiting for transfers between devices, body(): lax.psum_scatter(moe_grads, 'dp', scatter_dimension=0, tiled=True)  15 us
  transfers between devices with their start and end apart: 18, of which 17 were waited for; matrix products, arithmetic and copies ran while one was open for 25% of the time, Pallas kernels for 2%

profile of v1, /device:TPU:0, one launch (start us, length us, event | category | flops | bytes accessed | tf_op | source)
XLA Modules:
  0.0 573.0 jit_solution(14229509907111414975)
XLA Ops:
  7.2 1.8 stack_attention.1
  12.2 1.6 stack_experts.1
  18.8 6.5 %all-to-all-start = ((bf16[16,4,2176]{2,1,0:T(4,128)(2,1)}), bf16[16,4,2176]{2,1,0:T(4,128)(2,1)S(1)}, u32[]{:S(2)}, u32[]{:S(2)}) async-start(bf16[16,4,2176]{2,1,0:T(4,128)(2,1)} %pad_maximum_fusion.2), calls=%async_computation | async-start | bytes 557056 | tf_op jit(solution)/shard_map/all_to_all | solution.py:66
  26.8 2.2 multiply_cosine_fusion.1
  29.0 7.5 %all-to-all-done = bf16[16,4,2176]{2,1,0:T(4,128)(2,1)S(1)} async-done(((bf16[16,4,2176]{2,1,0:T(4,128)(2,1)}), bf16[16,4,2176]{2,1,0:T(4,128)(2,1)S(1)}, u32[]{:S(2)}, u32[]{:S(2)}) %all-to-all-start) | async-done | bytes 278560 | tf_op jit(solution)/shard_map/all_to_all | solution.py:66
  38.4 6.6 %all-to-all-start.1 = ((bf16[8,32,2048]{2,1,0:T(8,128)(2,1)}), bf16[8,32,2048]{2,1,0:T(8,128)(2,1)S(1)}, u32[]{:S(2)}, u32[]{:S(2)}) async-start(bf16[8,32,2048]{2,1,0:T(8,128)(2,1)} %broadcast_in_dim.115), calls=%async_computation.1 | async-start | bytes 2097152 | tf_op jit(solution)/shard_map/all_to_all | solution.py:66
  47.0 15.3 %all-to-all-done.1 = bf16[8,32,2048]{2,1,0:T(8,128)(2,1)S(1)} async-done(((bf16[8,32,2048]{2,1,0:T(8,128)(2,1)}), bf16[8,32,2048]{2,1,0:T(8,128)(2,1)S(1)}, u32[]{:S(2)}, u32[]{:S(2)}) %all-to-all-start.1) | async-done | bytes 1048608 | tf_op jit(solution)/shard_map/all_to_all | solution.py:66
  63.1 3.2 fusion.5
  67.2 6.0 %all-to-all-start.2 = ((f32[8,2,256]{2,1,0:T(2,128)}), f32[8,2,256]{2,1,0:T(2,128)S(1)}, u32[]{:S(2)}, u32[]{:S(2)}) async-start(f32[8,2,256]{2,1,0:T(2,128)} %broadcast_in_dim.116), calls=%async_computation.2 | async-start | bytes 32768 | tf_op jit(solution)/shard_map/all_to_all | solution.py:66
  74.3 6.6 %all-to-all-done.2 = f32[8,2,256]{2,1,0:T(2,128)S(1)} async-done(((f32[8,2,256]{2,1,0:T(2,128)}), f32[8,2,256]{2,1,0:T(2,128)S(1)}, u32[]{:S(2)}, u32[]{:S(2)}) %all-to-all-start.2) | async-done | bytes 16416 | tf_op jit(solution)/shard_map/all_to_all | solution.py:66
  85.2 4.2 all-to-all-start.3
  91.3 28.9 %all-to-all-done.3.packed = bf16[16,288,128]{2,1,0:T(8,128)(2,1)S(1)} async-done(((bf16[16,288,128]{2,1,0:T(8,128)(2,1)}), bf16[16,288,128]{2,1,0:T(8,128)(2,1)S(1)}, u32[]{:S(2)}, u32[]{:S(2)}) %all-to-all-start.3) | async-done | bytes 1179680 | tf_op jit(solution)/shard_map/all_to_all | solution.py:66
  120.2 3.0 attention.1
  123.2 11.0 %all_to_all.75 = bf16[16,32,128]{2,1,0:T(8,128)(2,1)S(1)} all-to-all(bf16[16,32,128]{2,1,0:T(8,128)(2,1)S(1)} %get-tuple-element.19), channel_id=1, replica_groups=mesh['dp'=16,'tensor'=8] {'dp'}, dimensions={0} | all-to-all | bytes 262144 | tf_op jit(solution)/shard_map/all_to_all | solution.py:66
  134.3 2.8 convolution_convert_fusion.2
  137.1 4.2 all-to-all-start.5
  141.5 18.6 %all-to-all-done.5 = bf16[8,32,2048]{2,1,0:T(8,128)(2,1)} async-done(((bf16[8,32,2048]{2,1,0:T(8,128)(2,1)}), bf16[8,32,2048]{2,1,0:T(8,128)(2,1)}, u32[]{:S(2)}, u32[]{:S(2)}) %all-to-all-start.5) | async-done | bytes 1048608 | tf_op jit(solution)/shard_map/all_to_all | solution.py:66
  161.2 4.2 all-to-all-start.7
  167.7 2.5 multiply_reduce_fusion.6
  176.8 7.1 %all-to-all-done.7 = bf16[8,32,2048]{2,1,0:T(8,128)(2,1)} async-done(((bf16[8,32,2048]{2,1,0:T(8,128)(2,1)}), bf16[8,32,2048]{2,1,0:T(8,128)(2,1)}, u32[]{:S(2)}, u32[]{:S(2)}) %all-to-all-start.7) | async-done | bytes 1048608 | tf_op jit(solution)/shard_map/all_to_all | solution.py:66
  183.9 2.0 broadcast_in_dim.132
  185.9 4.2 all-to-all-start.6
  195.9 2.3 copy.394
  198.1 10.5 %all-to-all-done.6 = bf16[8,32,2048]{2,1,0:T(8,128)(2,1)} async-done(((bf16[8,32,2048]{2,1,0:T(8,128)(2,1)}), bf16[8,32,2048]{2,1,0:T(8,128)(2,1)}, u32[]{:S(2)}, u32[]{:S(2)}) %all-to-all-start.6) | async-done | bytes 1048608 | tf_op jit(solution)/shard_map/all_to_all | solution.py:66
  208.6 2.3 copy.393
  210.9 32.3 %all-gather.5.cloned.1.call-done.weights = bf16[2048,6144]{1,0:T(8,128)(2,1)} async-done(((bf16[128,6144]{1,0:T(8,128)(2,1)}), bf16[2048,6144]{1,0:T(8,128)(2,1)}) %all-gather.5.cloned.1.call-update) | async-done | bytes 25165840 | tf_op jit(solution)/shard_map/all_gather | solution.py:387
  243.2 35.7 %experts.1 = (bf16[256,2048]{1,0:T(8,128)(2,1)}, bf16[256,2048]{1,0:T(8,128)(2,1)}, bf16[2048,6144]{1,0:T(8,128)(2,1)}) custom-call(bf16[256,2048]{1,0:T(8,128)(2,1)} %bitcast.39.rows, bf16[2048,256]{1,0:T(8,128)(2,1)} %bitcast.235, bf16[256,2048]{1,0:T(8,128)(2,1)} %bitcast.41.upstream, bf16[2048,256]{1,0:T(8,128)(2,1)} %bitcast.234, ...), custom_call_target="tpu_custom_call" | custom-call | tf_op jit(solution)/shard_map/experts/pallas_call | solution.py:258
  279.0 6.4 %all-to-all-start.8 = ((bf16[8,32,2048]{2,1,0:T(8,128)(2,1)}), bf16[8,32,2048]{2,1,0:T(8,128)(2,1)}, u32[]{:S(2)}, u32[]{:S(2)}) async-start(bf16[8,32,2048]{2,1,0:T(8,128)(2,1)} %bitcast.253), calls=%async_computation.8 | async-start | bytes 2097152 | tf_op jit(solution)/shard_map/all_to_all | solution.py:66
  286.6 15.7 %all-to-all-done.8 = bf16[8,32,2048]{2,1,0:T(8,128)(2,1)} async-done(((bf16[8,32,2048]{2,1,0:T(8,128)(2,1)}), bf16[8,32,2048]{2,1,0:T(8,128)(2,1)}, u32[]{:S(2)}, u32[]{:S(2)}) %all-to-all-start.8) | async-done | bytes 1048608 | tf_op jit(solution)/shard_map/all_to_all | solution.py:66
  302.3 2.1 convert_reduce_fusion.1
  304.4 1.8 reduce_sum.261
  306.2 2.0 multiply_reduce_fusion.5
  311.6 4.4 all-to-all-start.9
  316.2 17.3 %all-to-all-done.9 = bf16[8,32,2048]{2,1,0:T(8,128)(2,1)} async-done(((bf16[8,32,2048]{2,1,0:T(8,128)(2,1)}), bf16[8,32,2048]{2,1,0:T(8,128)(2,1)}, u32[]{:S(2)}, u32[]{:S(2)}) %all-to-all-start.9) | async-done | bytes 1048608 | tf_op jit(solution)/shard_map/all_to_all | solution.py:66
  333.5 2.1 convolution_convert_fusion.7
  336.3 4.5 all-to-all-start.10
  342.0 6.4 %all-to-all-done.10.delta_mixed = bf16[16,32,128]{2,1,0:T(8,128)(2,1)S(1)} async-done(((bf16[16,32,128]{2,1,0:T(8,128)(2,1)}), bf16[16,32,128]{2,1,0:T(8,128)(2,1)S(1)}, u32[]{:S(2)}, u32[]{:S(2)}) %all-to-all-start.10) | async-done | bytes 131104 | tf_op jit(solution)/shard_map/all_to_all | solution.py:66
  348.4 5.3 attention_back.1
  353.8 4.5 all-to-all-start.11
  361.4 2.4 reshape.958
  366.6 2.3 subtract_add_fusion
  368.8 14.9 %all-to-all-done.11 = bf16[16,288,128]{2,1,0:T(8,128)(2,1)} async-done(((bf16[16,288,128]{2,1,0:T(8,128)(2,1)}), bf16[16,288,128]{2,1,0:T(8,128)(2,1)}, u32[]{:S(2)}, u32[]{:S(2)}) %all-to-all-start.11) | async-done | bytes 1179680 | tf_op jit(solution)/shard_map/all_to_all | solution.py:66
  391.1 4.0 all-to-all-start.12
  397.1 5.7 all-to-all-done.12
  404.4 5.1 fusion.14
  412.5 3.6 fusion.13
  416.0 3.5 reshape.938
  419.5 3.8 add_convert_fusion.1
  423.3 3.4 fusion.7
  426.7 4.8 all-to-all-start.13
  433.6 2.3 copy.413
  435.9 1.7 convolution_convert_fusion.6
  440.0 2.2 convolution_convert_fusion.3
  442.2 2.6 fusion.1
  444.7 19.6 %all-to-all-done.13 = bf16[128,4,2176]{2,1,0:T(4,128)(2,1)S(1)} async-done(((bf16[128,4,2176]{2,1,0:T(4,128)(2,1)}), bf16[128,4,2176]{2,1,0:T(4,128)(2,1)S(1)}, u32[]{:S(2)}, u32[]{:S(2)}) %all-to-all-start.13) | async-done | bytes 2228256 | tf_op jit(solution)/shard_map/all_to_all | solution.py:66
  464.3 15.0 %reduce-scatter.3.cloned.1.call-done = bf16[128,6144]{1,0:T(8,128)(2,1)} async-done(((bf16[2048,6144]{1,0:T(8,128)(2,1)}), bf16[128,6144]{1,0:T(8,128)(2,1)}) %reduce-scatter.3.cloned.1.call-update) | async-done | bytes 1572880 | tf_op jit(solution)/shard_map/reduce_scatter | solution.py:484
  480.6 2.0 broadcast_in_dim.230
  482.6 7.2 %all-to-all-start.14 = ((bf16[8,16,4,2176]{3,2,1,0:T(4,128)(2,1)}), bf16[8,16,4,2176]{3,2,1,0:T(4,128)(2,1)S(1)}, u32[]{:S(2)}, u32[]{:S(2)}) async-start(bf16[8,16,4,2176]{3,2,1,0:T(4,128)(2,1)} %broadcast_in_dim.230), calls=%async_computation.14 | async-start | bytes 4456448 | tf_op jit(solution)/shard_map/all_to_all | solution.py:66
  490.2 24.6 %all-to-all-done.14 = bf16[8,16,4,2176]{3,2,1,0:T(4,128)(2,1)S(1)} async-done(((bf16[8,16,4,2176]{3,2,1,0:T(4,128)(2,1)}), bf16[8,16,4,2176]{3,2,1,0:T(4,128)(2,1)S(1)}, u32[]{:S(2)}, u32[]{:S(2)}) %all-to-all-start.14) | async-done | bytes 2228256 | tf_op jit(solution)/shard_map/all_to_all | solution.py:66
  514.9 2.5 fusion.49
  518.8 2.2 reshape.944
  525.1 4.1 reshape.963
  529.2 2.1 fusion.48
  535.2 27.2 %reduce-scatter.5.cloned.1.call-done = bf16[1,144,1024]{2,1,0:T(8,128)(2,1)} async-done(((bf16[16,144,1024]{2,1,0:T(8,128)(2,1)}), bf16[1,144,1024]{2,1,0:T(8,128)(2,1)}) %reduce-scatter.5.cloned.1.call-update) | async-done | bytes 294928 | tf_op jit(solution)/shard_map/reduce_scatter | solution.py:571
  (312 shorter events, 83.7 us)
Async XLA Ops:
  7.2 9.5 %copy-start = (bf16[2,128,2048]{2,1,0:T(8,128)(2,1)S(1)}, bf16[2,128,2048]{2,1,0:T(8,128)(2,1)}, u32[]{:S(2)}) copy-start(bf16[2,128,2048]{2,1,0:T(8,128)(2,1)} %param.18) | copy-start | bytes 3145732
  7.2 55.9 %all-gather.3.cloned.1.call-start = ((), (), s32[]{:S(2)}) async-start(), calls=%async_computation.17 | async-start | bytes 4456448 | tf_op jit(solution)/shard_map/all_gather | solution.py:321
  9.1 234.2 %all-gather.5.cloned.1.call-start = ((), (), s32[]{:S(2)}) async-start(), calls=%async_computation.18 | async-start | bytes 26738688 | tf_op jit(solution)/shard_map/all_gather | solution.py:387
  12.2 1.6 copy-start.61
  12.2 1.7 copy-start.62
  12.2 1.8 copy-start.35
  13.8 3.2 copy-start.15
  13.8 3.9 copy-start.59
  13.8 3.9 copy-start.60
  14.0 2.4 copy-start.52
  16.6 9.5 %copy-start.51 = (s32[2,2]{1,0:T(2,128)S(1)}, s32[2,2]{1,0:T(2,128)}, u32[]{:S(2)}) copy-start(s32[2,2]{1,0:T(2,128)} %param.20) | copy-start | bytes 52
  18.8 17.7 %all-to-all-start = ((bf16[16,4,2176]{2,1,0:T(4,128)(2,1)}), bf16[16,4,2176]{2,1,0:T(4,128)(2,1)S(1)}, u32[]{:S(2)}, u32[]{:S(2)}) async-start(bf16[16,4,2176]{2,1,0:T(4,128)(2,1)} %pad_maximum_fusion.2), calls=%async_computation | async-start | bytes 557056 | tf_op jit(solution)/shard_map/all_to_all | solution.py:66
  26.7 10.6 %copy-start.54 = (f32[64]{0:T(128)}, f32[64]{0:T(128)S(1)}, u32[]{:S(2)}) copy-start(f32[64]{0:T(128)S(1)} %negate_power_fusion) | copy-start | bytes 772
  26.8 11.6 %copy-start.16 = (f32[8,16,2]{2,1,0:T(8,128)}, f32[8,16,2]{2,1,0:T(8,128)S(1)}, u32[]{:S(2)}) copy-start(f32[8,16,2]{2,1,0:T(8,128)S(1)} %copy.375) | copy-start | bytes 3076
  36.5 9.9 %copy-start.12 = (bf16[16,4,2176]{2,1,0:T(4,128)(2,1)}, bf16[16,4,2176]{2,1,0:T(4,128)(2,1)S(1)}, u32[]{:S(2)}) copy-start(bf16[16,4,2176]{2,1,0:T(4,128)(2,1)S(1)} %all-to-all-done) | copy-start | bytes 835588
  38.4 23.9 %all-to-all-start.1 = ((bf16[8,32,2048]{2,1,0:T(8,128)(2,1)}), bf16[8,32,2048]{2,1,0:T(8,128)(2,1)S(1)}, u32[]{:S(2)}, u32[]{:S(2)}) async-start(bf16[8,32,2048]{2,1,0:T(8,128)(2,1)} %broadcast_in_dim.115), calls=%async_computation.1 | async-start | bytes 2097152 | tf_op jit(solution)/shard_map/all_to_all | solution.py:66
  47.0 19.3 %copy-start.33 = (f32[2048]{0:T(1024)}, f32[2048]{0:T(1024)S(1)}, u32[]{:S(2)}) copy-start(f32[2048]{0:T(1024)S(1)} %fusion.40) | copy-start | bytes 24580
  62.7 3.6 copy-start.47
  63.0 3.3 copy-start.7
  66.3 17.8 %copy-start.5 = (f32[256,768]{1,0:T(8,128)}, f32[256,768]{1,0:T(8,128)S(1)}, u32[]{:S(2)}) copy-start(f32[256,768]{1,0:T(8,128)S(1)} %fusion.5) | copy-start | bytes 2359300
  67.2 13.7 %all-to-all-start.2 = ((f32[8,2,256]{2,1,0:T(2,128)}), f32[8,2,256]{2,1,0:T(2,128)S(1)}, u32[]{:S(2)}, u32[]{:S(2)}) async-start(f32[8,2,256]{2,1,0:T(2,128)} %broadcast_in_dim.116), calls=%async_computation.2 | async-start | bytes 32768 | tf_op jit(solution)/shard_map/all_to_all | solution.py:66
  73.3 7.7 %copy-start.43 = (f32[256]{0:T(256)}, f32[256]{0:T(256)S(1)}, u32[]{:S(2)}) copy-start(f32[256]{0:T(256)S(1)} %reshape.954) | copy-start | bytes 3076
  73.5 7.6 %copy-start.45 = (f32[256]{0:T(256)}, f32[256]{0:T(256)S(1)}, u32[]{:S(2)}) copy-start(f32[256]{0:T(256)S(1)} %reshape.955) | copy-start | bytes 3076
  84.1 5.8 %copy-start.32 = (s32[2,16,128]{2,0,1:T(2,128)S(1)}, s32[2,16,128]{2,0,1:T(2,128)}, u32[]{:S(2)}) copy-start(s32[2,16,128]{2,0,1:T(2,128)} %copy-done.31) | copy-start | bytes 49156
  85.2 35.0 %all-to-all-start.3 = ((bf16[16,288,128]{2,1,0:T(8,128)(2,1)}), bf16[16,288,128]{2,1,0:T(8,128)(2,1)S(1)}, u32[]{:S(2)}, u32[]{:S(2)}) async-start(bf16[16,288,128]{2,1,0:T(8,128)(2,1)} %pad_maximum_fusion), calls=%async_computation.3 | async-start | bytes 2359296 | tf_op jit(solution)/shard_map/all_to_all | solution.py:66
  134.3 2.8 copy-start.13
  134.3 7.0 %copy-start.23 = (bf16[16,2,2048]{2,1,0:T(2,128)(2,1)S(1)}, bf16[16,2,2048]{2,1,0:T(2,128)(2,1)}, u32[]{:S(2)}) copy-start(bf16[16,2,2048]{2,1,0:T(2,128)(2,1)} %get-tuple-element.164) | copy-start | bytes 393220
  134.3 7.1 %copy-start.36 = (bf16[16,1,128]{2,1,0:T(2,128)(2,1)S(1)}, bf16[16,1,128]{2,1,0:T(2,128)(2,1)}, u32[]{:S(2)}) copy-start(bf16[16,1,128]{2,1,0:T(2,128)(2,1)} %get-tuple-element.166) | copy-start | bytes 12292
  137.1 22.9 %all-to-all-start.5 = ((bf16[8,32,2048]{2,1,0:T(8,128)(2,1)}), bf16[8,32,2048]{2,1,0:T(8,128)(2,1)}, u32[]{:S(2)}, u32[]{:S(2)}) async-start(bf16[8,32,2048]{2,1,0:T(8,128)(2,1)} %bitcast.236), calls=%async_computation.5 | async-start | bytes 2097152 | tf_op jit(solution)/shard_map/all_to_all | solution.py:66
  161.2 22.8 %all-to-all-start.7 = ((bf16[8,32,2048]{2,1,0:T(8,128)(2,1)}), bf16[8,32,2048]{2,1,0:T(8,128)(2,1)}, u32[]{:S(2)}, u32[]{:S(2)}) async-start(bf16[8,32,2048]{2,1,0:T(8,128)(2,1)} %broadcast_in_dim.134), calls=%async_computation.7 | async-start | bytes 2097152 | tf_op jit(solution)/shard_map/all_to_all | solution.py:66
  185.9 22.7 %all-to-all-start.6 = ((bf16[8,32,2048]{2,1,0:T(8,128)(2,1)}), bf16[8,32,2048]{2,1,0:T(8,128)(2,1)}, u32[]{:S(2)}, u32[]{:S(2)}) async-start(bf16[8,32,2048]{2,1,0:T(8,128)(2,1)} %broadcast_in_dim.132), calls=%async_computation.6 | async-start | bytes 2097152 | tf_op jit(solution)/shard_map/all_to_all | solution.py:66
  190.2 289.2 %reduce-scatter.3.cloned.1.call-start = ((), (), s32[]{:S(2)}) async-start(), calls=%async_computation.19 | async-start | bytes 26738688 | tf_op jit(solution)/shard_map/reduce_scatter | solution.py:484
  279.0 23.3 %all-to-all-start.8 = ((bf16[8,32,2048]{2,1,0:T(8,128)(2,1)}), bf16[8,32,2048]{2,1,0:T(8,128)(2,1)}, u32[]{:S(2)}, u32[]{:S(2)}) async-start(bf16[8,32,2048]{2,1,0:T(8,128)(2,1)} %bitcast.253), calls=%async_computation.8 | async-start | bytes 2097152 | tf_op jit(solution)/shard_map/all_to_all | solution.py:66
  310.5 5.5 copy-start.17
  311.6 21.8 %all-to-all-start.9 = ((bf16[8,32,2048]{2,1,0:T(8,128)(2,1)}), bf16[8,32,2048]{2,1,0:T(8,128)(2,1)}, u32[]{:S(2)}, u32[]{:S(2)}) async-start(bf16[8,32,2048]{2,1,0:T(8,128)(2,1)} %broadcast_in_dim.226), calls=%async_computation.9 | async-start | bytes 2097152 | tf_op jit(solution)/shard_map/all_to_all | solution.py:66
  316.1 24.7 %copy-start.55 = (f32[64]{0:T(128)S(1)}, f32[64]{0:T(128)}, u32[]{:S(2)}) copy-start(f32[64]{0:T(128)} %copy-done.54) | copy-start | bytes 772
  336.3 12.1 %all-to-all-start.10 = ((bf16[16,32,128]{2,1,0:T(8,128)(2,1)}), bf16[16,32,128]{2,1,0:T(8,128)(2,1)S(1)}, u32[]{:S(2)}, u32[]{:S(2)}) async-start(bf16[16,32,128]{2,1,0:T(8,128)(2,1)} %bitcast.51), calls=%async_computation.10 | async-start | bytes 262144 | tf_op jit(solution)/shard_map/all_to_all | solution.py:66
  353.7 5.1 copy-start.24
  353.7 5.1 copy-start.25
  353.7 5.9 %copy-start.48 = (f32[256]{0:T(256)S(1)}, f32[256]{0:T(256)}, u32[]{:S(2)}) copy-start(f32[256]{0:T(256)} %copy-done.47) | copy-start | bytes 3076
  353.7 6.4 %copy-start.38 = (f32[1,256]{1,0:T(1,128)S(1)}, f32[1,256]{1,0:T(1,128)}, u32[]{:S(2)}) copy-start(f32[1,256]{1,0:T(1,128)} %copy-done.37) | copy-start | bytes 3076
  353.7 6.4 %copy-start.41 = (f32[1,256]{1,0:T(1,128)S(1)}, f32[1,256]{1,0:T(1,128)}, u32[]{:S(2)}) copy-start(f32[1,256]{1,0:T(1,128)} %copy-done.40) | copy-start | bytes 3076
  353.8 7.0 %copy-start.50 = (f32[16,2]{0,1:T(2,128)S(1)}, f32[16,2]{0,1:T(2,128)}, u32[]{:S(2)}) copy-start(f32[16,2]{0,1:T(2,128)} %get-tuple-element.192) | copy-start | bytes 388
  353.8 30.0 %all-to-all-start.11 = ((bf16[16,288,128]{2,1,0:T(8,128)(2,1)}), bf16[16,288,128]{2,1,0:T(8,128)(2,1)}, u32[]{:S(2)}, u32[]{:S(2)}) async-start(bf16[16,288,128]{2,1,0:T(8,128)(2,1)} %attention_back.1), calls=%async_computation.11 | async-start | bytes 2359296 | tf_op jit(solution)/shard_map/all_to_all | solution.py:66
  358.3 8.2 %copy-start.10 = (f32[16,2,2048]{2,1,0:T(2,128)S(1)}, f32[16,2,2048]{2,1,0:T(2,128)}, u32[]{:S(2)}) copy-start(f32[16,2,2048]{2,1,0:T(2,128)} %get-tuple-element.146) | copy-start | bytes 786436
  358.3 8.2 %copy-start.30 = (f32[16,2]{1,0:T(8,128)S(1)}, f32[16,2]{1,0:T(8,128)}, u32[]{:S(2)}) copy-start(f32[16,2]{1,0:T(8,128)} %copy.391) | copy-start | bytes 388
  389.0 15.4 %copy-start.34 = (f32[2048]{0:T(1024)S(1)}, f32[2048]{0:T(1024)}, u32[]{:S(2)}) copy-start(f32[2048]{0:T(1024)} %copy-done.33) | copy-start | bytes 24580
  391.1 11.7 %all-to-all-start.12 = ((f32[8,2,256]{2,1,0:T(2,128)}), f32[8,2,256]{2,1,0:T(2,128)S(1)}, u32[]{:S(2)}, u32[]{:S(2)}) async-start(f32[8,2,256]{2,1,0:T(2,128)} %broadcast_in_dim.227), calls=%async_computation.12 | async-start | bytes 32768 | tf_op jit(solution)/shard_map/all_to_all | solution.py:66
  404.3 5.1 copy-start.18
  404.4 8.1 %copy-start.49 = (f32[256]{0:T(256)S(1)}, f32[256]{0:T(256)}, u32[]{:S(2)}) copy-start(f32[256]{0:T(256)} %copy-done.47) | copy-start | bytes 3076
  416.0 3.5 copy-start.58
  419.5 3.8 copy-start.26
  426.7 4.9 copy-start.8
  426.7 37.6 %all-to-all-start.13 = ((bf16[128,4,2176]{2,1,0:T(4,128)(2,1)}), bf16[128,4,2176]{2,1,0:T(4,128)(2,1)S(1)}, u32[]{:S(2)}, u32[]{:S(2)}) async-start(bf16[128,4,2176]{2,1,0:T(4,128)(2,1)} %bitcast.233), calls=%async_computation.13 | async-start | bytes 4456448 | tf_op jit(solution)/shard_map/all_to_all | solution.py:66
  431.5 130.8 %reduce-scatter.5.cloned.1.call-start = ((), (), s32[]{:S(2)}) async-start(), calls=%async_computation.20 | async-start | bytes 5013504 | tf_op jit(solution)/shard_map/reduce_scatter | solution.py:571
  433.6 4.0 copy-start.57
  433.6 4.7 copy-start.56
  433.6 6.3 %copy-start.19 = (bf16[256,256]{1,0:T(8,128)(2,1)S(1)}, bf16[256,256]{1,0:T(8,128)(2,1)}, u32[]{:S(2)}) copy-start(bf16[256,256]{1,0:T(8,128)(2,1)} %copy-done.18) | copy-start | bytes 393220
  482.6 7.2 %copy-start.29 = (s32[2,16,8]{2,1,0:T(8,128)S(1)}, s32[2,16,8]{2,1,0:T(8,128)}, u32[]{:S(2)}) copy-start(s32[2,16,8]{2,1,0:T(8,128)} %copy-done.28) | copy-start | bytes 3076
  482.6 7.2 %copy-start.53 = (s32[2]{0:T(128)S(1)}, s32[2]{0:T(128)}, u32[]{:S(2)}) copy-start(s32[2]{0:T(128)} %copy-done.52) | copy-start | bytes 28
  482.6 32.2 %all-to-all-start.14 = ((bf16[8,16,4,2176]{3,2,1,0:T(4,128)(2,1)}), bf16[8,16,4,2176]{3,2,1,0:T(4,128)(2,1)S(1)}, u32[]{:S(2)}, u32[]{:S(2)}) async-start(bf16[8,16,4,2176]{3,2,1,0:T(4,128)(2,1)} %broadcast_in_dim.230), calls=%async_computation.14 | async-start | bytes 4456448 | tf_op jit(solution)/shard_map/all_to_all | solution.py:66
  521.0 2.7 copy-start.9
  531.3 2.6 copy-start.11
  533.9 32.3 %copy-start.1 = (bf16[2,128,2048]{2,1,0:T(8,128)(2,1)S(1)}, bf16[2,128,2048]{2,1,0:T(8,128)(2,1)}, u32[]{:S(2)}) copy-start(bf16[2,128,2048]{2,1,0:T(8,128)(2,1)} %param.18) | copy-start | bytes 3145732
  (17 other events, 19.1 us)
Sparse Core Ops, SparseCore 0:
  10.3 51.8 all-gather.2
  63.9 179.2 all-gather.4
  279.1 200.1 reduce-scatter.2
  481.6 80.6 reduce-scatter.4
